TPU v7x, 256 devices: a whole 4x4x8 slice. The times are simulated.
256 devices in a mesh: tm: 8 (over x, core), src: 32 (over z, y).
Axes of the slice: x: 4, y: 4, z: 8, core: 2. Of those that a mesh axis runs over, the one named last changes fastest.
Arguments:
- src_deriv: bfloat16 [32768, 5, 128], P(('tm', 'src')), may hold values from -6 to 6
- att_deriv: bfloat16 [32768, 12, 128], P(('tm', 'src')), may hold values from -6 to 6
- cal_deriv: bfloat16 [32768, 24, 128], P(('tm', 'src')), may hold values from -6 to 6
- obs_resid: float32 [32768, 128], P(('tm', 'src')), may hold values from -8 to 8
- obs_weight: float32 [32768, 128], P(('tm', 'src')), may hold values from 0.25 to 4
- src_id: int32 [32768], P(('tm', 'src')), may hold values from 0 to 1023
- tile_knot: int32 [32768], P(('tm', 'src')), may hold values from 0 to 32761, as said below
- row_offset: int32 [32768, 128], P(('tm', 'src')), may hold values from 0 to 3
- cal_unit: int32 [32768], P(('tm', 'src')), may hold values from 0 to 63
- src_prior: float32 [5, 32768], P(None, 'src'), may hold values from 100 to 1000
- att_ridge: float32 [98304], P('tm'), may hold values from 100 to 1000
Outputs:
- source_update: float32 [5, 32768], P(None, 'src')
- attitude_update: float32 [98304], P('tm')
- calib_update: float32 [24, 64], replicated
- residual_out: float32 [32768, 128], P(('tm', 'src'))
Inputs may be any that keep to these rules, and one draw needn't show every extreme that they name: `tile_knot`: tile t belongs to time slab t // 4096; its knot lies in that slab's knots, from slab * 4096 to slab * 4096 + 4095, and is at most 32761.
All inputs are finite; a program needn't handle non-finite values.
Results may differ from a plain program's by a relative error of at most 0.0003.
Values sent between devices are 32-bit elements; how exact they have to be, the bound alone decides.
A program may use at most 128 MiB of HBM per device.

v0:
```python
import functools

import jax
import jax.numpy as jnp
import numpy as np
from jax import lax
from jax.experimental import pallas as pl
from jax.experimental.pallas import tpu as pltpu
from jax.sharding import PartitionSpec as P

NCU = 64
CG_ITERS = 6


HIGH = lax.Precision.HIGHEST


def padded_2(cells, sides, width):
    for axis, dim in sides:
        count = lax.axis_size(axis)
        ends = count - 1
        head = lax.slice_in_dim(cells, 0, width, axis=dim)
        tail = lax.slice_in_dim(cells, cells.shape[dim] - width, cells.shape[dim], axis=dim)
        cells = jnp.concatenate(
            [
                lax.ppermute(tail, axis, [(i, (i + 1) % count) for i in range(ends)]),
                cells,
                lax.ppermute(head, axis, [((i + 1) % count, i) for i in range(ends)]),
            ],
            axis=dim,
        )
    return cells


def all_sum(array, axis):
    devices, step = lax.axis_size(axis), 1
    while step < devices:
        array = array + lax.ppermute(array, axis, [(i, i ^ step) for i in range(devices)])
        step *= 2
    return array


def from_behind(array, axis, by):
    devices = lax.axis_size(axis)
    pairs = [(i, i + by) for i in range(devices) if 0 <= i + by < devices]
    return lax.ppermute(array, axis, pairs)


def lag_table():
    first_index = np.arange(21)[None, :]
    lag_rows = np.arange(12)[:, None]
    second = first_index + lag_rows
    flat_index = first_index * 21 + np.minimum(second, 20)
    return (flat_index, (second < 21).astype(np.float32))


def solve_spd(matrix, right):
    order = right.shape[0]
    rows = jnp.arange(order)[:, None]

    def column(j, state):
        rest, factor = state
        col = jnp.where(rows >= j, rest[:, j] / jnp.sqrt(rest[j, j]), 0.0)
        return rest - col[:, None, :] * col[None, :, :], factor.at[:, j].set(col)

    factor = lax.fori_loop(0, order, column, (matrix, jnp.zeros_like(matrix)))[1]

    def forward(i, answer):
        value = right[i] - jnp.sum(jnp.where(rows < i, factor[i] * answer, 0.0), axis=0)
        return answer.at[i].set(value / factor[i, i])

    halfway = lax.fori_loop(0, order, forward, jnp.zeros_like(right))

    def backward(step, answer):
        i = order - 1 - step
        value = halfway[i] - jnp.sum(jnp.where(rows > i, factor[:, i] * answer, 0.0), axis=0)
        return answer.at[i].set(value / factor[i, i])

    return lax.fori_loop(0, order, backward, jnp.zeros_like(right))


def tile_normals(deriv, weight, resid):
    values = deriv.astype(jnp.float32)
    weighted = values * weight[:, None, :]
    normal = jnp.einsum("tkr,tlr->tkl", weighted, values, precision=HIGH)
    right = jnp.einsum("tkr,tr->tk", weighted, resid, precision=HIGH)
    return jnp.concatenate([normal.reshape(normal.shape[0], -1), right], axis=1)


def small_solve(sums, prior, order):
    count = sums.shape[1]
    matrix = sums[: order * order].reshape(order, order, count)
    if prior is not None:
        matrix = matrix + jnp.eye(order, dtype=jnp.float32)[:, :, None] * prior[:, None, :]
    return solve_spd(matrix, sums[order * order :])


def window_rows(att_deriv, row_offset):
    values = att_deriv.astype(jnp.float32)
    window = jnp.zeros((values.shape[0], 21, values.shape[2]), jnp.float32)
    for knot_step in range(4):
        placed = jnp.pad(values, ((0, 0), (3 * knot_step, 9 - 3 * knot_step), (0, 0)))
        window = window + jnp.where((row_offset == knot_step)[:, None, :], placed, 0.0)
    return window


def attitude_terms(window, weight, resid):
    weighted = window * weight[:, None, :]
    normal = jnp.einsum("tjr,tlr->tjl", weighted, window, precision=HIGH)
    right = jnp.einsum("tjr,tr->tj", weighted, resid, precision=HIGH)
    flat_index, valid_lag = lag_table()
    banded = normal.reshape(normal.shape[0], 441)[:, flat_index] * valid_lag
    return jnp.concatenate([banded, right[:, None, :]], axis=1)


def conjugate(band_rows, right, ridge_part, band_edge, extend, inner_sum):
    count = right.shape[0]
    lagged = jnp.concatenate([band_edge, band_rows[1:]], axis=1)
    solution = jnp.zeros_like(right)
    residual = right
    direction = right
    norm_now = inner_sum(residual, residual)
    for iteration in range(CG_ITERS):
        padded = extend(direction)
        result = ridge_part * direction
        for d in range(12):
            result = result + band_rows[d] * padded[11 + d : 11 + d + count]
        for d in range(1, 12):
            result = (
                result + lagged[d - 1, 11 - d : 11 - d + count] * padded[11 - d : 11 - d + count]
            )
        step_size = norm_now / inner_sum(direction, result)
        solution = solution + step_size * direction
        residual = residual - step_size * result
        norm_next = inner_sum(residual, residual)
        direction = residual + norm_next / norm_now * direction
        norm_now = norm_next
    return solution


def slab_extend(vector):
    return padded_2(vector, (("tm", 0),), 11)


def slab_dot(first_vec, second_vec):
    return all_sum(jnp.sum(first_vec * second_vec), "tm")


def shards(
    src_deriv,
    att_deriv,
    cal_deriv,
    obs_resid,
    obs_weight,
    src_id,
    tile_knot,
    row_offset,
    cal_unit,
    src_prior,
    att_ridge,
):
    slab_pos = lax.axis_index("tm")
    groups = src_prior.shape[1]
    normal_sums = jax.ops.segment_sum(
        tile_normals(src_deriv, obs_weight, obs_resid), src_id, num_segments=groups
    ).T
    summed = all_sum(normal_sums, "tm")
    source_update = small_solve(summed, src_prior, 5)
    resid_a = obs_resid - jnp.einsum(
        "tkr,kt->tr", src_deriv.astype(jnp.float32), source_update[:, src_id], precision=HIGH
    )
    slab_params = att_ridge.shape[0]
    window = window_rows(att_deriv, row_offset)
    local_knot = tile_knot - slab_pos * (slab_params // 3)
    columns = 3 * local_knot[:, None] + jnp.arange(21, dtype=jnp.int32)[None, :]
    values = attitude_terms(window, obs_weight, resid_a)
    slab_sums = jax.ops.segment_sum(
        values.transpose(0, 2, 1).reshape(-1, 13),
        columns.reshape(-1),
        num_segments=slab_params + 21,
    ).T
    carried = from_behind(slab_sums[:, slab_params:], "tm", 1)
    head_sums = slab_sums[:, :slab_params].at[:, :21].add(carried)
    summed_band = all_sum(head_sums, "src")
    band_edge = from_behind(summed_band[1:12, -11:], "tm", 1)
    attitude_update = conjugate(
        summed_band[:12], summed_band[12], att_ridge, band_edge, slab_extend, slab_dot
    )
    next_params = from_behind(attitude_update[:21], "tm", -1)
    extended = jnp.concatenate([attitude_update, next_params])
    resid_b = resid_a - jnp.einsum("tjr,tj->tr", window, extended[columns], precision=HIGH)
    calib_sums = jax.ops.segment_sum(
        tile_normals(cal_deriv, obs_weight, resid_b), cal_unit, num_segments=NCU
    ).T
    calib_total = all_sum(all_sum(calib_sums, "tm"), "src")
    calib_update = small_solve(calib_total, None, 24)
    residual_out = resid_b - jnp.einsum(
        "tkr,kt->tr", cal_deriv.astype(jnp.float32), calib_update[:, cal_unit], precision=HIGH
    )
    return (source_update, attitude_update, calib_update, residual_out)


F32 = jnp.float32
BF16 = jnp.bfloat16
MESH = pl.DeviceIdType.MESH
MROWS = 32
XROWS = 24
TRUST = 0.01


def pieces_2(x):
    high = x.astype(BF16)
    return high, (x - high.astype(F32)).astype(BF16)


def pieces_3(x):
    high = x.astype(BF16)
    rest = x - high.astype(F32)
    mid = rest.astype(BF16)
    return high, mid, (rest - mid.astype(F32)).astype(BF16)


def dot_nn(a, b):
    return lax.dot_general(a, b, (((1,), (0,)), ((), ())), preferred_element_type=F32)


def dot_nt(a, b):
    return lax.dot_general(a, b, (((1,), (1,)), ((), ())), preferred_element_type=F32)


def iota(shape, dim):
    return lax.broadcasted_iota(jnp.int32, shape, dim)


def hot(match):
    return jnp.where(match, 1.0, 0.0).astype(BF16)


def band_slots():
    slots = [(0, c, d) for c in range(3) for d in range(c, 3)]
    for delta in range(1, 4):
        slots += [(delta, c, d) for c in range(3) for d in range(3)]
    return slots


SLOTS = band_slots()
SLOT_AT = {slot: v for v, slot in enumerate(SLOTS)}
SRC_PAIRS = [(k, l) for k in range(5) for l in range(k, 5)]
SRC_AT = {pair: e for e, pair in enumerate(SRC_PAIRS)}
GRAM_PAIRS = [(i, j) for i in range(CG_ITERS) for j in range(i, CG_ITERS)]


def cal_row(k, l):
    if k < 8:
        return 24 * k + l
    if k < 16:
        return 192 + 16 * (k - 8) + l - 8
    return 320 + 8 * (k - 16) + l - 16


def place_lanes(lo_row):
    inside = iota((128, 128), 0) - lo_row
    return inside, iota((8, 128), 0) + 128 - lo_row


def ldl_solve(entry, right, order):
    low = {}
    pivots, inverse, shares = [], [], []
    for j in range(order):
        pivot = entry(j, j)
        for m in range(j):
            pivot = pivot - low[j, m] * low[j, m] * pivots[m]
        shares.append(pivot / entry(j, j))
        pivots.append(pivot)
        inverse.append(1.0 / pivot)
        for i in range(j + 1, order):
            value = entry(j, i)
            for m in range(j):
                value = value - low[i, m] * (low[j, m] * pivots[m])
            low[i, j] = value * inverse[j]
    forward = []
    for i in range(order):
        value = right(i)
        for m in range(i):
            value = value - low[i, m] * forward[m]
        forward.append(value)
    answer = [None] * order
    for i in range(order - 1, -1, -1):
        value = forward[i] * inverse[i]
        for m in range(i + 1, order):
            value = value - low[m, i] * answer[m]
        answer[i] = value
    return answer, shares


def joint_kernel(
    n_tm,
    n_src,
    n_hi,
    src_ref,
    att_in_ref,
    cal_ref,
    resid_in_ref,
    weight_ref,
    offset_ref,
    meta_ref,
    prior_ref,
    ridge_ref,
    update_ref,
    att_ref,
    calib_ref,
    resid_ref,
    trust_ref,
    winp,
    srcp,
    calp,
    offp,
    w_ref,
    r_ref,
    vm,
    vc,
    vs,
    mb,
    ex,
    cp,
    vsr,
    mr,
    mown,
    halo,
    band,
    pb,
    br,
    basis,
    image,
    gs,
    g1,
    g2,
    gt,
    xm,
    xr,
    sub,
    cr,
    c2s,
    c2r,
    c3s,
    cf,
    inv,
    ra,
    vrow,
    kz,
    ky,
    kt,
    ks,
    send,
    recv,
):
    tm, sr = lax.axis_index("tm"), lax.axis_index("src")
    last_tm, last_sr = n_tm - 1, n_src - 1
    has_next, has_prev = tm < last_tm, tm > 0
    first, final = sr == 0, sr == last_sr
    ny = min(4, n_src)
    nz = n_src // ny
    yy, zz = sr % ny, sr // ny
    per_own = 24 // min(24, n_src)
    n_own = 24 // per_own
    share = 8 * per_own
    owner = sr < n_own
    lanes = prior_ref.shape[1] // n_tm

    def start(source, target, at, place):
        pltpu.make_async_remote_copy(
            src_ref=source,
            dst_ref=target,
            send_sem=send.at[at],
            recv_sem=recv.at[at],
            device_id=place,
            device_id_type=MESH,
        ).start()

    def arrived(part, at):
        pltpu.make_async_copy(part, part, recv.at[at]).wait()

    def left_us(part, at):
        pltpu.make_async_copy(part, part, send.at[at]).wait()

    def each(count, body):
        def run(d, carry):
            body(d)
            return carry

        lax.fori_loop(0, count, run, 0)

    def other_src(body):
        each(last_sr, lambda d: body((sr + 1 + d) % n_src))

    def other_tm(body):
        each(last_tm, lambda d: body((tm + 1 + d) % n_tm))

    halo[...] = jnp.zeros_like(halo)
    xr[...] = jnp.zeros_like(xr)

    barrier = pltpu.get_barrier_semaphore()

    def greet(a, b):
        pl.semaphore_signal(barrier, inc=1, device_id=(a, b), device_id_type=MESH)

    other_tm(lambda p: greet(p, sr))
    other_src(lambda p: greet(tm, p))
    next_tm, prev_tm = jnp.minimum(tm + 1, last_tm), jnp.maximum(tm - 1, 0)
    pl.when(has_next)(lambda: greet(next_tm, 0))
    pl.when(has_prev)(lambda: greet(prev_tm, last_sr))
    pl.when(has_prev & first)(lambda: each(n_src, lambda i: greet(prev_tm, i)))
    pl.when(has_next & final)(lambda: each(n_src, lambda i: greet(next_tm, i)))

    w_ref[...] = weight_ref[...].T
    r_ref[...] = resid_in_ref[...].T
    offp[...] = offset_ref[...].astype(F32).T.astype(jnp.int32)
    vm[...] = jnp.zeros_like(vm)
    pb[...] = jnp.zeros_like(pb)

    def windows(i, carry):
        rows = pl.ds(pl.multiple_of(i * 16, 16), 16)
        values = [att_in_ref[k, rows, :].astype(F32) for k in range(12)]
        step = offp[rows, :]
        for j in range(21):
            placed = jnp.zeros((16, 128), F32)
            for o in range(4):
                if 0 <= j - 3 * o < 12:
                    placed = jnp.where(step == o, values[j - 3 * o], placed)
            winp[j, rows, :] = placed
        for k in range(5):
            srcp[k, rows, :] = src_ref[k, rows, :].astype(F32)
        return carry

    lax.fori_loop(0, 8, windows, 0)

    def summed(count, terms):
        def body(i, sums):
            rows = pl.ds(pl.multiple_of(i * 8, 8), 8)
            return tuple(s + t for s, t in zip(sums, terms(rows)))

        sums = lax.fori_loop(0, 16, body, tuple(jnp.zeros((8, 128), F32) for _ in range(count)))
        return [jnp.sum(s, axis=0, keepdims=True) for s in sums]

    def src_terms(rows):
        x = [srcp[k, rows, :] for k in range(5)]
        w = w_ref[rows, :]
        y = [w * v for v in x]
        r = r_ref[rows, :]
        return [y[k] * x[l] for k, l in SRC_PAIRS] + [v * r for v in y]

    vs[...] = jnp.zeros_like(vs)
    for e, row in enumerate(summed(20, src_terms)):
        vs[e : e + 1, :] = row
    vs[20:21, :] = meta_ref[0:1, :].astype(F32)

    trace = jnp.sum(ridge_ref[...], axis=0, keepdims=True) * (1.0 / n_src)
    for m in range(7):
        slots = [s for s in SLOTS if m + s[0] < 7]

        def att_terms(rows, m=m, slots=slots):
            x = [winp[j, rows, :] for j in range(3 * m, min(3 * m + 12, 21))]
            w = w_ref[rows, :]
            y = [w * x[c] for c in range(3)]
            return [y[c] * x[3 * delta + d] for delta, c, d in slots]

        for slot, row in zip(slots, summed(len(slots), att_terms)):
            vm[m, SLOT_AT[slot] : SLOT_AT[slot] + 1, :] = row
            if slot[0] == 0 and slot[1] == slot[2]:
                trace = trace + row
    vs[21:22, :] = trace

    knot = meta_ref[1:2, :]
    block, place = knot >> 7, knot & 127
    inside, past = place_lanes(place)
    blocks = iota((n_hi + 8, 128), 0)
    here, after = hot(blocks == block), hot(blocks == block + 1)
    spreads = jnp.concatenate([here, here, after, after], axis=1)
    rest = jnp.zeros((120, 128), F32)

    def spread_rows(row_of, count):
        spread = jnp.zeros((128, 128), F32)
        over = jnp.zeros((8, 128), F32)
        for m in range(count):
            row = row_of(m)
            spread = jnp.where(inside == m, row, spread)
            over = jnp.where(past == m, row, over)
        over = jnp.concatenate([over, rest], axis=0)
        right = jnp.concatenate(pieces_2(spread) + pieces_2(over), axis=1)
        return dot_nt(spreads, right)[:n_hi]

    callers = last_tm + last_sr + jnp.where(has_next, 1, 0) + jnp.where(has_prev, 1, 0)
    callers = callers + jnp.where(has_prev & first, n_src, 0) + jnp.where(has_next & final, n_src, 0)
    pl.semaphore_wait(barrier, callers)

    other_tm(lambda p: start(vs, vsr.at[tm], 0, (p, sr)))

    for v, (delta, c, d) in enumerate(SLOTS):
        rows = spread_rows(lambda m, v=v: vm[m, v : v + 1, :], 7 - delta)
        if v < MROWS:
            mb[pl.ds(v, n_hi, stride=MROWS), :] = rows
        else:
            ex[...] = rows

    def band_rows(j):
        return mb.at[pl.ds(pl.multiple_of(j * MROWS, 8), MROWS)]

    other_src(lambda p: start(band_rows(p), mr.at[sr], 1, (tm, p)))
    pl.when(has_next)(lambda: start(band_rows(n_src), mr.at[n_src + sr], 2, (next_tm, 0)))

    def widen(i, carry):
        rows = pl.ds(pl.multiple_of(i * 16, 16), 16)
        for k in range(24):
            calp[k, rows, :] = cal_ref[k, rows, :].astype(F32)
        return carry

    lax.fori_loop(0, 8, widen, 0)
    for kg in range(6):
        for lg in range(kg // 2, 3):

            def cal_terms(rows, kg=kg, lg=lg):
                w = w_ref[rows, :]
                y = [w * calp[4 * kg + k, rows, :] for k in range(4)]
                x = [calp[8 * lg + l, rows, :] for l in range(8)]
                return [y[k] * x[l] for k in range(4) for l in range(8)]

            sums = summed(32, cal_terms)
            for k in range(4):
                at = cal_row(4 * kg + k, 8 * lg)
                vc[at : at + 8, :] = jnp.concatenate(sums[8 * k : 8 * k + 8], axis=0)
    unit_hot = hot(iota((NCU, 128), 0) == meta_ref[2:3, :])
    unit_hot_2 = jnp.concatenate([unit_hot, unit_hot], axis=1)
    units = dot_nt(jnp.concatenate(pieces_2(vc[...]), axis=1), unit_hot_2)
    cp[...] = jnp.concatenate([units[:192], units[192:]], axis=1)

    def cal_share(p):
        return cp.at[pl.ds(pl.multiple_of(p * share, 8), share)]

    def send_cal(p):
        pl.when(p < n_own)(lambda: start(cal_share(p), cr.at[sr], 3, (tm, p)))

    other_src(send_cal)

    ids = jnp.broadcast_to(meta_ref[0:1, :].astype(F32), (128, 128)).T
    sources = (iota((lanes, 128), 0) + tm * lanes).astype(F32)
    wanted = jnp.concatenate([ids, sources], axis=0)
    flat_at, plane_at = iota((384, 384), 1), iota((384, 384), 0)
    mixed = hot(flat_at == 3 * (plane_at & 127) + (plane_at >> 7))
    flat_ridge = jnp.concatenate([ridge_ref[pl.ds(3 * sr + q, 1), :] for q in range(3)], axis=1)
    ridge_row = sum(dot_nt(jnp.broadcast_to(part, (16, 384)), mixed)[0:1] for part in pieces_3(flat_ridge))
    groups = prior_ref.shape[1]
    source_hot = hot(iota((groups, 128), 0) == meta_ref[0:1, :])
    owned = dot_nn(jnp.concatenate(pieces_3(prior_ref[...]), axis=0), source_hot)
    owned = owned[0:8] + owned[8:16] + owned[16:24]

    vsr[tm] = vs[...]
    arrived(vsr.at[pl.ds(0, last_tm)], 0)
    normal = jnp.zeros((48, 128 + lanes), F32)
    for p in range(0, n_tm, 2):
        match = [hot(wanted == vsr[q, 20:21, :]) for q in (p, p + 1)]
        parts = [pieces_2(vsr[q]) for q in (p, p + 1)]
        left = jnp.concatenate([jnp.concatenate([part[i] for part in parts], axis=1) for i in range(2)], axis=0)
        normal = normal + dot_nt(left, jnp.concatenate(match, axis=1))
    normal = normal[:24] + normal[24:]
    trace = sum(vsr[p, 21:22, :] for p in range(n_tm))
    prior = jnp.concatenate([owned, prior_ref[:, pl.ds(pl.multiple_of(tm * lanes, 128), lanes)]], axis=1)

    def source_entry(k, l):
        row = SRC_AT[k, l]
        value = normal[row : row + 1]
        return value + prior[k : k + 1] if k == l else value

    update, _ = ldl_solve(source_entry, lambda k: normal[15 + k : 16 + k], 5)
    resid_a = r_ref[...]
    for k in range(5):
        resid_a = resid_a - srcp[k] * update[k][:, :128]
    ra[...] = resid_a
    weighted = w_ref[...] * resid_a
    for j in range(21):
        vrow[j : j + 1, :] = jnp.sum(winp[j] * weighted, axis=0, keepdims=True)

    lane = iota((n_hi, 128), 1)

    def put_blocks(rows, centre_at, edge_at, extra=None):
        edges = jnp.where(lane < 64, pltpu.roll(rows, n_hi - 1, 0), pltpu.roll(rows, 1, 0))
        if extra is not None:
            edges = jnp.where((lane == 64) & (iota((n_hi, 128), 0) < n_src), extra, edges)
        pb[pl.ds(centre_at, n_hi, stride=8), :] = rows
        pb[pl.ds(edge_at, n_hi, stride=8), :] = edges

    trace = jnp.sum(trace, axis=1, keepdims=True)
    for c in range(3):
        rows = spread_rows(lambda m, c=c: vrow[3 * m + c : 3 * m + c + 1, :], 7)
        put_blocks(rows, c, 3 + c, trace if c == 0 else None)
    put_blocks(ex[...], 6, 7)

    def right_rows(j):
        return pb.at[pl.ds(pl.multiple_of(j * 8, 8), 8)]

    other_src(lambda p: start(right_rows(p), br.at[sr], 4, (tm, p)))
    pl.when(has_next)(lambda: start(right_rows(n_src), br.at[n_src + sr], 5, (next_tm, 0)))
    pl.when(has_prev)(lambda: start(right_rows(n_hi - 1), br.at[n_src + sr], 6, (prev_tm, last_sr)))

    for k in range(5):
        sub[tm, k : k + 1, :] = update[k][:, 128:]
    other_tm(lambda p: start(sub.at[tm], sub.at[tm], 7, (p, sr)))

    mr[sr] = mb[pl.ds(pl.multiple_of(sr * MROWS, 8), MROWS), :]
    arrived(mr.at[pl.ds(0, last_sr)], 1)
    total = mr[0]
    for i in range(1, n_src):
        total = total + mr[i]
    mown[...] = total

    def add_carried():
        arrived(mr.at[pl.ds(n_src, n_src)], 2)
        total = mown[...]
        for i in range(n_src):
            total = total + mr[n_src + i]
        mown[...] = total

    pl.when(has_prev & first)(add_carried)
    for c in range(3):
        v = SLOT_AT[0, c, c]
        mown[v : v + 1, :] = mown[v : v + 1, :] + ridge_row[:, 128 * c : 128 * c + 128]
    lin = tm * n_src + sr
    lower, upper = jnp.maximum(lin - 1, 0), jnp.minimum(lin + 1, n_tm * n_src - 1)
    has_left, has_right = lin > 0, lin < n_tm * n_src - 1
    pl.when(has_left)(lambda: start(mown, halo.at[1], 8, (lower // n_src, lower % n_src)))
    pl.when(has_right)(lambda: start(mown, halo.at[0], 9, (upper // n_src, upper % n_src)))

    def sum_cal():
        cr[sr] = cp[pl.ds(pl.multiple_of(sr * share, 8), share), :]
        arrived(cr.at[pl.ds(0, last_sr)], 3)
        total = cr[0]
        for i in range(1, n_src):
            total = total + cr[i]
        c2s[...] = total
        c2r[tm] = total
        other_tm(lambda p: start(c2s, c2r.at[tm], 10, (p, sr)))

    pl.when(owner)(sum_cal)

    pl.when(has_left)(lambda: arrived(halo.at[0], 9))
    pl.when(has_right)(lambda: arrived(halo.at[1], 8))
    def finish_cal():
        arrived(c2r.at[pl.ds(0, last_tm)], 10)
        total = c2r[0]
        for i in range(1, n_tm):
            total = total + c2r[i]
        c3s[...] = total
        cf[sr] = total
        other_src(lambda p: start(c3s, cf.at[sr], 11, (tm, p)))

    pl.when(owner)(finish_cal)

    br[sr] = pb[pl.ds(pl.multiple_of(sr * 8, 8), 8), :]
    arrived(br.at[pl.ds(0, last_sr)], 4)
    basis[0] = jnp.zeros((8, 384), F32)
    total = br[0]
    for i in range(1, n_src):
        total = total + br[i]
    gt[0:8, :] = total
    trace = total[3:4, 64:65]

    def add_other(at):
        arrived(br.at[pl.ds(n_src, n_src)], at)
        total = gt[0:8, :]
        for i in range(n_src):
            total = total + br[n_src + i]
        gt[0:8, :] = total

    pl.when(has_prev & first)(lambda: add_other(5))
    pl.when(has_next & final)(lambda: add_other(6))
    lane = iota((8, 128), 1)

    def widened(centre, edge):
        return jnp.concatenate([jnp.where(lane >= 110, edge, 0.0), centre, jnp.where(lane < 18, edge, 0.0)], axis=1)

    total = gt[0:8, :]
    edge = jnp.concatenate([total[3:8], total[0:3]], axis=0)
    basis[1] = jnp.where(iota((8, 384), 0) < 3, widened(total, edge), 0.0)
    last = widened(total[6:7] + jnp.zeros((8, 128), F32), total[7:8] + jnp.zeros((8, 128), F32))[0:1]
    full = jnp.concatenate([halo[0], mown[...], halo[1]], axis=1)
    full = jnp.concatenate([full, jnp.broadcast_to(last, (8, 384))], axis=0)
    band[...] = jnp.zeros_like(band)
    for d in range(3):
        for c in range(3):
            v = SLOT_AT[0, min(c, d), max(c, d)]
            band[9 + d, c : c + 1, :] = full[v : v + 1]
    for delta in range(1, 4):
        base = SLOT_AT[delta, 0, 0]
        moved = pltpu.roll(full, delta, 1)
        for d in range(3):
            for c in range(3):
                v = base + 3 * c + d
                band[3 * (3 + delta) + d, c : c + 1, :] = full[v : v + 1]
                v = base + 3 * d + c
                band[3 * (3 - delta) + d, c : c + 1, :] = moved[v : v + 1]

    mean = trace * (1.0 / (384 * n_src * n_tm))
    centre = jnp.broadcast_to(mean * 1.2, (8, 384))
    scale = jnp.broadcast_to(2.0 / (mean * 1.1), (8, 384))

    def grow(k, carry):
        x = basis[k + 1]
        y = jnp.zeros((8, 384), F32)
        for delta in range(-3, 4):
            moved = x if delta == 0 else pltpu.roll(x, (-delta) % 384, 1)
            for d in range(3):
                y = y + band[3 * (3 + delta) + d] * moved[d : d + 1]
        image[k] = y[:, 128:256]
        basis[k + 2] = scale * (y - centre * x) - basis[k]
        return carry

    lax.fori_loop(0, CG_ITERS, grow, 0)
    own = [basis[k + 1][:, 128:256] for k in range(CG_ITERS)]
    images = [image[k] for k in range(CG_ITERS)]
    rows = [jnp.sum(own[i] * images[j], axis=0, keepdims=True) for i, j in GRAM_PAIRS]
    rows += [jnp.sum(own[0] * own[i], axis=0, keepdims=True) for i in range(CG_ITERS)]
    for e, row in enumerate(rows):
        gt[e : e + 1, :] = row
    n_gram = len(rows)
    in_gram = iota((32, 128), 0) < n_gram
    same = iota((32, 128), 0) == iota((32, 128), 1)
    sums = jnp.sum(jnp.where(in_gram, gt[...], 0.0), axis=1, keepdims=True)
    gs[0] = jnp.broadcast_to(jnp.sum(jnp.where(same, sums, 0.0), axis=0, keepdims=True), (8, 128))
    g1[sr] = gs[0]
    other_src(lambda p: start(gs.at[0], g1.at[sr], 12, (tm, p)))
    for k in range(CG_ITERS):
        xm[3 * k : 3 * k + 3, :] = own[k][0:3]

    def slab_rows(i):
        return xr.at[pl.ds(pl.multiple_of(i * XROWS, 8), XROWS)]

    other_src(lambda p: start(xm, slab_rows(sr), 14, (tm, p)))
    pl.when(has_prev & first)(
        lambda: each(n_src, lambda i: start(xm, slab_rows(n_src), 15, (prev_tm, i)))
    )
    xr[pl.ds(pl.multiple_of(sr * XROWS, 8), XROWS), :] = xm[...]

    pl.when(owner)(lambda: arrived(cf.at[pl.ds(0, n_own - 1)], 11))
    pl.when(jnp.logical_not(owner))(lambda: arrived(cf, 11))
    packed = jnp.concatenate([cf[i] for i in range(n_own)], axis=0)
    other_half = pltpu.roll(packed, 64, 1)
    for k in range(24):
        size = 24 - 8 * (k // 8)
        at = cal_row(k, 8 * (k // 8))
        part = packed[at : at + size] if k < 8 else other_half[at - 192 : at - 192 + size]
        inv[24 * k + 8 * (k // 8) : 24 * k + 24, :] = part
    for k in range(8, 24):
        size = 8 * (k // 8)
        inv[24 * k : 24 * k + size, :] = inv[pl.ds(k, size, stride=24), :]

    def sweep(j, carry):
        row_of = iota((24, 128), 0)
        column = inv[pl.ds(pl.multiple_of(24 * j, 8), 24), :]
        pivot = jnp.sum(jnp.where(row_of == j, column, 0.0), axis=0, keepdims=True)
        over = 1.0 / pivot
        scaled = column * over
        for k in range(24):
            at = inv[24 * k : 24 * k + 24, :]
            factor = scaled[k : k + 1]
            inv[24 * k : 24 * k + 24, :] = jnp.where(row_of == j, factor, at - factor * column)
        inv[pl.ds(pl.multiple_of(24 * j, 8), 24), :] = jnp.where(row_of == j, -over, scaled)
        return carry

    lax.fori_loop(0, 12, sweep, 0)

    arrived(g1.at[pl.ds(0, last_sr)], 12)
    total = g1[0]
    for i in range(1, n_src):
        total = total + g1[i]
    gs[1] = total
    g2[tm] = total
    other_tm(lambda p: start(gs.at[1], g2.at[tm], 13, (p, sr)))
    lax.fori_loop(12, 24, sweep, 0)
    arrived(g2.at[pl.ds(0, last_tm)], 13)
    total = g2[0]
    for i in range(1, n_tm):
        total = total + g2[i]
    sums = jnp.sum(jnp.where(same, total[0:1], 0.0), axis=1, keepdims=True)
    gt[...] = jnp.broadcast_to(sums, (32, 128))
    gram_at = {pair: e for e, pair in enumerate(GRAM_PAIRS)}
    n_pairs = len(GRAM_PAIRS)

    def gram(i, j):
        e = gram_at[i, j]
        return gt[e : e + 1, :]

    weights, shares = ldl_solve(gram, lambda i: gt[n_pairs + i : n_pairs + i + 1, :], CG_ITERS)
    least = shares[0]
    for value in shares[1:]:
        least = jnp.where(value >= least, least, value)
    trust_ref[...] = jnp.broadcast_to(jnp.where(least > TRUST, 1.0, 0.0), (8, 128))
    arrived(sub.at[pl.ds(0, last_tm)], 7)
    for p in range(n_tm):
        update_ref[:, lanes * p : lanes * p + lanes] = sub[p, 0:5, :]

    here_3 = jnp.concatenate([here[:n_hi].astype(F32)] * 3 + [jnp.zeros((128 - 3 * n_hi, 128), F32)], axis=0).astype(BF16)
    after_3 = jnp.concatenate([after[:n_hi].astype(F32)] * 3 + [jnp.zeros((128 - 3 * n_hi, 128), F32)], axis=0).astype(BF16)
    arrived(xr.at[pl.ds(0, XROWS * last_sr)], 14)
    pl.when(has_next)(lambda: arrived(slab_rows(n_src), 15))
    resid_b = ra[...]
    planes = []
    for c in range(3):
        plane = weights[0] * xr[pl.ds(c, n_hi, stride=XROWS), :]
        for k in range(1, CG_ITERS):
            plane = plane + weights[k] * xr[pl.ds(3 * k + c, n_hi, stride=XROWS), :]
        planes.append(plane)
        parts = [part.astype(F32) for part in pieces_3(plane)]
        parts.append(jnp.zeros((128 - 3 * n_hi, 128), F32))
        turned = jnp.concatenate(parts, axis=0).T.astype(BF16)
        at_place = dot_nn(turned, here_3)
        past_place = dot_nn(turned[:16], after_3)[:8]
        for m in range(7):
            value = jnp.sum(jnp.where(inside == m, at_place, 0.0), axis=0, keepdims=True)
            value = value + jnp.sum(jnp.where(past == m, past_place, 0.0), axis=0, keepdims=True)
            resid_b = resid_b - winp[3 * m + c] * value

    weighted = w_ref[...] * resid_b
    for k in range(24):
        vrow[k : k + 1, :] = jnp.sum(calp[k] * weighted, axis=0, keepdims=True)
    units = dot_nt(jnp.concatenate(pieces_2(vrow[...]), axis=1), unit_hot_2)
    ks[0, 0:8, :] = jnp.concatenate([units[0:8], units[8:16]], axis=1)
    ks[0, 8:16, :] = jnp.concatenate([units[16:24], jnp.zeros((8, NCU), F32)], axis=1)

    def exchange(buffer, count, me, at, place, beside=None):
        buffer[me] = ks[at]
        each(
            count - 1,
            lambda d: start(ks.at[at], buffer.at[me], 16 + at, place((me + 1 + d) % count)),
        )
        if beside is not None:
            beside()
        arrived(buffer.at[pl.ds(0, count - 1)], 16 + at)
        total = buffer[0]
        for i in range(1, count):
            total = total + buffer[i]
        ks[at + 1] = total

    def write_attitude():
        slab = jnp.concatenate(planes, axis=1)
        flat = dot_nn(jnp.concatenate(pieces_3(slab), axis=0), mixed)
        flat = flat[:n_hi] + flat[n_hi : 2 * n_hi] + flat[2 * n_hi :]
        for q in range(3):
            att_ref[pl.ds(q, n_src, stride=3), :] = flat[:n_src, 128 * q : 128 * q + 128]

    exchange(kz, nz, zz, 0, lambda p: (tm, p * ny + yy), write_attitude)
    exchange(ky, ny, yy, 1, lambda p: (tm, zz * ny + p))
    exchange(kt, n_tm, tm, 2, lambda p: (p, sr))
    total = ks[3]
    right = jnp.concatenate([total[0:8, :NCU], total[0:8, NCU:], total[8:16, :NCU]], axis=0)
    calib = jnp.zeros((24, NCU), F32)
    for j in range(24):
        calib = calib - inv[24 * j : 24 * j + 24, :NCU] * right[j : j + 1]
    calib_ref[...] = calib
    spread = dot_nn(jnp.concatenate(pieces_3(calib), axis=0), unit_hot)
    spread = spread[0:24] + spread[24:48] + spread[48:72]
    out = resid_b
    for k in range(24):
        out = out - calp[k] * spread[k : k + 1]
    resid_ref[...] = out.T

    left_us(vsr.at[pl.ds(0, last_tm)], 0)
    left_us(mr.at[pl.ds(0, last_sr)], 1)
    pl.when(has_next)(lambda: left_us(mr.at[0], 2))
    pl.when(owner)(lambda: left_us(cr.at[pl.ds(0, n_own - 1)], 3))
    pl.when(jnp.logical_not(owner))(lambda: left_us(cr.at[pl.ds(0, n_own)], 3))
    left_us(br.at[pl.ds(0, last_sr)], 4)
    pl.when(has_next)(lambda: left_us(br.at[0], 5))
    pl.when(has_prev)(lambda: left_us(br.at[0], 6))
    left_us(sub.at[pl.ds(0, last_tm)], 7)
    pl.when(has_left)(lambda: left_us(mown, 8))
    pl.when(has_right)(lambda: left_us(mown, 9))
    pl.when(owner)(lambda: left_us(c2r.at[pl.ds(0, last_tm)], 10))
    pl.when(owner)(lambda: left_us(cr.at[pl.ds(0, last_sr)], 11))
    left_us(g1.at[pl.ds(0, last_sr)], 12)
    left_us(g2.at[pl.ds(0, last_tm)], 13)
    left_us(xr.at[pl.ds(0, XROWS * last_sr)], 14)
    pl.when(has_prev & first)(lambda: left_us(xr.at[pl.ds(0, XROWS * n_src)], 15))
    left_us(kz.at[pl.ds(0, nz - 1)], 16)
    left_us(ky.at[pl.ds(0, ny - 1)], 17)
    left_us(kt.at[pl.ds(0, last_tm)], 18)


def fast_shards(
    n_tm,
    n_src,
    src_deriv,
    att_deriv,
    cal_deriv,
    obs_resid,
    obs_weight,
    src_id,
    tile_knot,
    row_offset,
    cal_unit,
    src_prior,
    att_ridge,
):
    n_hi = (n_src + 1 + 7) // 8 * 8
    groups = src_prior.shape[1]
    lanes = groups // n_tm
    per_own = 24 // min(24, n_src)
    n_own, share = 24 // per_own, 8 * (24 // min(24, n_src))
    ny = min(4, n_src)
    nz = n_src // ny
    src_planes = jnp.transpose(src_deriv, (1, 2, 0))
    att_planes = jnp.transpose(att_deriv, (1, 2, 0))
    cal_planes = jnp.transpose(cal_deriv, (1, 2, 0))
    local_knot = tile_knot - lax.axis_index("tm") * (128 * n_src)
    meta = jnp.stack([src_id, local_knot, cal_unit] + [jnp.zeros_like(src_id)] * 5)
    ridge = att_ridge.reshape(3 * n_src, 128)
    prior = jnp.concatenate([src_prior, jnp.ones((3, groups), F32)], axis=0)

    def f32(*shape):
        return jax.ShapeDtypeStruct(shape, F32)

    def vmem(*shape):
        return pltpu.VMEM(shape, F32)

    whole = pl.BlockSpec(memory_space=pltpu.VMEM)
    return pl.pallas_call(
        functools.partial(joint_kernel, n_tm, n_src, n_hi),
        out_shape=[f32(5, groups), f32(3 * n_src, 128), f32(24, NCU), f32(128, 128), f32(8, 128)],
        in_specs=[whole] * 9,
        out_specs=[whole] * 5,
        scratch_shapes=[
            vmem(21, 128, 128),
            vmem(5, 128, 128),
            vmem(24, 128, 128),
            pltpu.VMEM((128, 128), jnp.int32),
            vmem(128, 128),
            vmem(128, 128),
            vmem(7, MROWS + 8, 128),
            vmem(384, 128),
            vmem(24, 128),
            vmem(n_hi * MROWS, 128),
            vmem(n_hi, 128),
            vmem(192, 128),
            vmem(n_tm, 24, 128),
            vmem(2 * n_src, MROWS, 128),
            vmem(MROWS, 128),
            vmem(2, MROWS, 128),
            vmem(21, 8, 384),
            vmem(n_hi * 8, 128),
            vmem(2 * n_src, 8, 128),
            vmem(CG_ITERS + 2, 8, 384),
            vmem(CG_ITERS, 8, 128),
            vmem(2, 8, 128),
            vmem(n_src, 8, 128),
            vmem(n_tm, 8, 128),
            vmem(32, 128),
            vmem(XROWS, 128),
            vmem(n_hi * XROWS, 128),
            vmem(n_tm, 8, lanes),
            vmem(n_src, share, 128),
            vmem(share, 128),
            vmem(n_tm, share, 128),
            vmem(share, 128),
            vmem(n_own, share, 128),
            vmem(576, 128),
            vmem(128, 128),
            vmem(24, 128),
            vmem(nz, 16, 128),
            vmem(ny, 16, 128),
            vmem(n_tm, 16, 128),
            vmem(4, 16, 128),
            pltpu.SemaphoreType.DMA((19,)),
            pltpu.SemaphoreType.DMA((19,)),
        ],
        compiler_params=pltpu.CompilerParams(
            collective_id=0, has_side_effects=True, vmem_limit_bytes=48 << 20
        ),
        name="joint_solve",
    )(src_planes, att_planes, cal_planes, obs_resid, obs_weight, row_offset, meta, prior, ridge)


def guarded_shards(n_tm, n_src, *arrays):
    update, attitude, calib, resid, trust = fast_shards(n_tm, n_src, *arrays)
    fast = (update, attitude.reshape(-1), calib, resid)
    return lax.cond(trust[0, 0] > 0.5, lambda: fast, lambda: shards(*arrays))


def solution(mesh):
    placed = (
        P(("tm", "src"), None, None),
        P(("tm", "src"), None, None),
        P(("tm", "src"), None, None),
        P(("tm", "src"), None),
        P(("tm", "src"), None),
        P(("tm", "src")),
        P(("tm", "src")),
        P(("tm", "src"), None),
        P(("tm", "src")),
        P(None, "src"),
        P("tm"),
    )
    return jax.shard_map(
        functools.partial(guarded_shards, mesh.shape["tm"], mesh.shape["src"]),
        mesh=mesh,
        in_specs=placed,
        out_specs=(P(None, "src"), P("tm"), P(), P(("tm", "src"), None)),
        check_vma=False,
    )
```

profile of v0, /device:TPU:1, one launch (start us, length us, event | category | flops | bytes accessed | tf_op | source)
XLA Modules:
  0.0 82.2 jit_solution(5052862437689609853)
XLA Ops:
  0.6 0.0 copy-start.4
  0.6 0.0 copy-start.1
  0.7 0.0 copy-start.13
  0.7 0.0 copy-start.27
  0.7 0.0 copy-start.25
  0.7 0.0 copy-start.28
  0.7 0.0 copy-start.10
  0.7 0.0 copy-start.8
  0.7 0.0 copy-start.7
  0.7 0.0 copy-start.9
  0.7 1.7 %copy.103 = bf16[128,24,128]{0,2,1:T(8,128)(2,1)S(1)} copy(bf16[128,24,128]{2,1,0:T(8,128)(2,1)} %param.44) | data formatting | bytes 1572864 | tf_op args[2]
  2.4 0.0 copy-start
  2.4 0.0 copy-done.4
  2.4 0.2 copy.102
  2.7 0.0 copy-done.1
  2.7 0.2 copy.101
  2.9 0.0 copy-done.13
  2.9 0.0 copy-done.27
  2.9 0.0 copy-done.25
  2.9 0.0 copy-done.28
  3.0 0.0 copy-done.10
  3.0 0.0 copy-done.8
  3.0 0.0 copy-done.7
  3.0 0.0 copy-done.9
  3.0 73.7 %joint_solve.1 = (f32[5,1024]{1,0:T(8,128)S(1)}, f32[96,128]{1,0:T(8,128)S(1)}, f32[24,64]{1,0:T(8,128)}, f32[128,128]{1,0:T(8,128)}, f32[8,128]{1,0:T(8,128)S(1)}) custom-call(bf16[5,128,128]{2,1,0:T(8,128)(2,1)S(1)} %bitcast.218, bf16[12,128,128]{2,1,0:T(8,128)(2,1)S(1)} %bitcast.217, bf16[24,128,128]{2,1,0:T(8,128)(2,1)S(1)} %bitcast.216, ...), custom_call_target="tpu_custom_call" | custom-call | tf_op jit(solution)/shard_map/joint_solve/pallas_call | solution.py:924
  76.7 0.5 slice.997
  77.9 0.0 copy-done
  77.9 0.2 conditional.1
  78.1 0.6 copy.204
  78.8 0.6 copy.205
  79.4 1.3 %copy.206 = f32[24,64]{1,0:T(8,128)} copy(f32[24,64]{1,0:T(8,128)} %get-tuple-element.1419) | data formatting | bytes 12288
  80.7 1.5 %copy.207 = f32[128,128]{1,0:T(8,128)} copy(f32[128,128]{1,0:T(8,128)} %get-tuple-element.1420) | data formatting | bytes 131072
  (5 shorter events, 0.0 us)
Async XLA Ops:
  0.6 1.8 %copy-start.4 = (bf16[128,12,128]{2,0,1:T(8,128)(2,1)S(1)}, bf16[128,12,128]{2,0,1:T(8,128)(2,1)}, u32[]{:S(2)}) copy-start(bf16[128,12,128]{2,0,1:T(8,128)(2,1)} %param.43) | copy-start | bytes 1179652
  0.6 2.0 %copy-start.1 = (bf16[128,5,128]{2,0,1:T(8,128)(2,1)S(1)}, bf16[128,5,128]{2,0,1:T(8,128)(2,1)}, u32[]{:S(2)}) copy-start(bf16[128,5,128]{2,0,1:T(8,128)(2,1)} %param.42) | copy-start | bytes 491524
  0.7 2.2 %copy-start.13 = (f32[5,1024]{1,0:T(8,128)S(1)}, f32[5,1024]{1,0:T(8,128)}, u32[]{:S(2)}) copy-start(f32[5,1024]{1,0:T(8,128)} %param.51) | copy-start | bytes 61444
  0.7 2.2 %copy-start.27 = (s32[128]{0:T(128)S(1)}, s32[128]{0:T(128)}, u32[]{:S(2)}) copy-start(s32[128]{0:T(128)} %param.48) | copy-start | bytes 1540
  0.7 2.2 %copy-start.25 = (s32[128]{0:T(128)S(1)}, s32[128]{0:T(128)}, u32[]{:S(2)}) copy-start(s32[128]{0:T(128)} %param.47) | copy-start | bytes 1540
  0.7 2.2 %copy-start.28 = (s32[128]{0:T(128)S(1)}, s32[128]{0:T(128)}, u32[]{:S(2)}) copy-start(s32[128]{0:T(128)} %param.50) | copy-start | bytes 1540
  0.7 2.3 %copy-start.10 = (f32[12288]{0:T(1024)S(1)}, f32[12288]{0:T(1024)}, u32[]{:S(2)}) copy-start(f32[12288]{0:T(1024)} %param.52) | copy-start | bytes 147460
  0.7 2.3 %copy-start.8 = (f32[128,128]{1,0:T(8,128)S(1)}, f32[128,128]{1,0:T(8,128)}, u32[]{:S(2)}) copy-start(f32[128,128]{1,0:T(8,128)} %resid_in_ref.1) | copy-start | bytes 196612
  0.7 2.3 %copy-start.7 = (f32[128,128]{1,0:T(8,128)S(1)}, f32[128,128]{1,0:T(8,128)}, u32[]{:S(2)}) copy-start(f32[128,128]{1,0:T(8,128)} %weight_ref.1) | copy-start | bytes 196612
  0.7 2.3 %copy-start.9 = (s32[128,128]{1,0:T(8,128)S(1)}, s32[128,128]{1,0:T(8,128)}, u32[]{:S(2)}) copy-start(s32[128,128]{1,0:T(8,128)} %offset_ref.1) | copy-start | bytes 196612
  2.4 75.5 %copy-start = (bf16[128,24,128]{2,1,0:T(8,128)(2,1)S(1)}, bf16[128,24,128]{2,1,0:T(8,128)(2,1)}, u32[]{:S(2)}) copy-start(bf16[128,24,128]{2,1,0:T(8,128)(2,1)} %param.44) | copy-start | bytes 2359300
where the time goes:
time: 82.4 us; the launch traced here: 82.2 us
  Pallas kernels  73.7 us (89%)
  local copies, waits for them, and re-layouts  6.69 us (8%)
  between operations  1.52 us (2%)
    pallas_call x1, Pallas kernels, fast_shards(): pl.pallas_call(functools.partial(joint_kernel, n_tm, n_src, n_hi), out_sh...  73.7 us
    unnamed x29, local copies, waits for them, and re-layouts  6.14 us

commit v1 on v0

--- a/solution.py
+++ b/solution.py
@@ -303,17 +303,22 @@
     resid_in_ref,
     weight_ref,
     offset_ref,
-    meta_ref,
-    prior_ref,
+    id_ref,
+    knot_ref,
+    unit_ref,
+    raw_prior_ref,
     ridge_ref,
     update_ref,
     att_ref,
     calib_ref,
     resid_ref,
     trust_ref,
+    prior_ref,
     winp,
     srcp,
+    attp,
     calp,
+    calf,
     offp,
     w_ref,
     r_ref,
@@ -396,8 +401,9 @@
     def other_tm(body):
         each(last_tm, lambda d: body((tm + 1 + d) % n_tm))
 
+    next_tm, prev_tm = jnp.minimum(tm + 1, last_tm), jnp.maximum(tm - 1, 0)
     halo[...] = jnp.zeros_like(halo)
-    xr[...] = jnp.zeros_like(xr)
+    xr[XROWS * n_src :, :] = jnp.zeros((XROWS * (n_hi - n_src), 128), F32)
 
     barrier = pltpu.get_barrier_semaphore()
 
@@ -406,21 +412,22 @@
 
     other_tm(lambda p: greet(p, sr))
     other_src(lambda p: greet(tm, p))
-    next_tm, prev_tm = jnp.minimum(tm + 1, last_tm), jnp.maximum(tm - 1, 0)
-    pl.when(has_next)(lambda: greet(next_tm, 0))
-    pl.when(has_prev)(lambda: greet(prev_tm, last_sr))
-    pl.when(has_prev & first)(lambda: each(n_src, lambda i: greet(prev_tm, i)))
-    pl.when(has_next & final)(lambda: each(n_src, lambda i: greet(next_tm, i)))
 
     w_ref[...] = weight_ref[...].T
     r_ref[...] = resid_in_ref[...].T
     offp[...] = offset_ref[...].astype(F32).T.astype(jnp.int32)
+    for k in range(5):
+        srcp[k] = src_ref[k].astype(F32)
+    for k in range(12):
+        attp[k] = att_in_ref[k].astype(F32)
     vm[...] = jnp.zeros_like(vm)
+    prior_ref[...] = jnp.ones_like(prior_ref)
+    prior_ref[0:5, :] = raw_prior_ref[...]
     pb[...] = jnp.zeros_like(pb)
 
     def windows(i, carry):
         rows = pl.ds(pl.multiple_of(i * 16, 16), 16)
-        values = [att_in_ref[k, rows, :].astype(F32) for k in range(12)]
+        values = [attp[k, rows, :] for k in range(12)]
         step = offp[rows, :]
         for j in range(21):
             placed = jnp.zeros((16, 128), F32)
@@ -428,8 +435,6 @@
                 if 0 <= j - 3 * o < 12:
                     placed = jnp.where(step == o, values[j - 3 * o], placed)
             winp[j, rows, :] = placed
-        for k in range(5):
-            srcp[k, rows, :] = src_ref[k, rows, :].astype(F32)
         return carry
 
     lax.fori_loop(0, 8, windows, 0)
@@ -452,7 +457,7 @@
     vs[...] = jnp.zeros_like(vs)
     for e, row in enumerate(summed(20, src_terms)):
         vs[e : e + 1, :] = row
-    vs[20:21, :] = meta_ref[0:1, :].astype(F32)
+    vs[20:21, :] = id_ref[...].astype(F32)
 
     trace = jnp.sum(ridge_ref[...], axis=0, keepdims=True) * (1.0 / n_src)
     for m in range(7):
@@ -470,7 +475,7 @@
                 trace = trace + row
     vs[21:22, :] = trace
 
-    knot = meta_ref[1:2, :]
+    knot = knot_ref[...] - tm * (128 * n_src)
     block, place = knot >> 7, knot & 127
     inside, past = place_lanes(place)
     blocks = iota((n_hi + 8, 128), 0)
@@ -489,12 +494,6 @@
         right = jnp.concatenate(pieces_2(spread) + pieces_2(over), axis=1)
         return dot_nt(spreads, right)[:n_hi]
 
-    callers = last_tm + last_sr + jnp.where(has_next, 1, 0) + jnp.where(has_prev, 1, 0)
-    callers = callers + jnp.where(has_prev & first, n_src, 0) + jnp.where(has_next & final, n_src, 0)
-    pl.semaphore_wait(barrier, callers)
-
-    other_tm(lambda p: start(vs, vsr.at[tm], 0, (p, sr)))
-
     for v, (delta, c, d) in enumerate(SLOTS):
         rows = spread_rows(lambda m, v=v: vm[m, v : v + 1, :], 7 - delta)
         if v < MROWS:
@@ -505,56 +504,21 @@
     def band_rows(j):
         return mb.at[pl.ds(pl.multiple_of(j * MROWS, 8), MROWS)]
 
-    other_src(lambda p: start(band_rows(p), mr.at[sr], 1, (tm, p)))
-    pl.when(has_next)(lambda: start(band_rows(n_src), mr.at[n_src + sr], 2, (next_tm, 0)))
-
-    def widen(i, carry):
-        rows = pl.ds(pl.multiple_of(i * 16, 16), 16)
-        for k in range(24):
-            calp[k, rows, :] = cal_ref[k, rows, :].astype(F32)
-        return carry
-
-    lax.fori_loop(0, 8, widen, 0)
-    for kg in range(6):
-        for lg in range(kg // 2, 3):
-
-            def cal_terms(rows, kg=kg, lg=lg):
-                w = w_ref[rows, :]
-                y = [w * calp[4 * kg + k, rows, :] for k in range(4)]
-                x = [calp[8 * lg + l, rows, :] for l in range(8)]
-                return [y[k] * x[l] for k in range(4) for l in range(8)]
-
-            sums = summed(32, cal_terms)
-            for k in range(4):
-                at = cal_row(4 * kg + k, 8 * lg)
-                vc[at : at + 8, :] = jnp.concatenate(sums[8 * k : 8 * k + 8], axis=0)
-    unit_hot = hot(iota((NCU, 128), 0) == meta_ref[2:3, :])
-    unit_hot_2 = jnp.concatenate([unit_hot, unit_hot], axis=1)
-    units = dot_nt(jnp.concatenate(pieces_2(vc[...]), axis=1), unit_hot_2)
-    cp[...] = jnp.concatenate([units[:192], units[192:]], axis=1)
-
-    def cal_share(p):
-        return cp.at[pl.ds(pl.multiple_of(p * share, 8), share)]
-
-    def send_cal(p):
-        pl.when(p < n_own)(lambda: start(cal_share(p), cr.at[sr], 3, (tm, p)))
-
-    other_src(send_cal)
-
-    ids = jnp.broadcast_to(meta_ref[0:1, :].astype(F32), (128, 128)).T
+    ids = jnp.broadcast_to(id_ref[...].astype(F32), (128, 128)).T
     sources = (iota((lanes, 128), 0) + tm * lanes).astype(F32)
     wanted = jnp.concatenate([ids, sources], axis=0)
-    flat_at, plane_at = iota((384, 384), 1), iota((384, 384), 0)
-    mixed = hot(flat_at == 3 * (plane_at & 127) + (plane_at >> 7))
-    flat_ridge = jnp.concatenate([ridge_ref[pl.ds(3 * sr + q, 1), :] for q in range(3)], axis=1)
-    ridge_row = sum(dot_nt(jnp.broadcast_to(part, (16, 384)), mixed)[0:1] for part in pieces_3(flat_ridge))
     groups = prior_ref.shape[1]
-    source_hot = hot(iota((groups, 128), 0) == meta_ref[0:1, :])
+    source_hot = hot(iota((groups, 128), 0) == id_ref[...])
     owned = dot_nn(jnp.concatenate(pieces_3(prior_ref[...]), axis=0), source_hot)
     owned = owned[0:8] + owned[8:16] + owned[16:24]
 
+    pl.semaphore_wait(barrier, last_tm + last_sr)
+    other_tm(lambda p: start(vs, vsr.at[tm], 0, (p, sr)))
+    other_src(lambda p: start(band_rows(p), mr.at[sr], 1, (tm, p)))
+
     vsr[tm] = vs[...]
     arrived(vsr.at[pl.ds(0, last_tm)], 0)
+    pl.when(has_next)(lambda: start(band_rows(n_src), mr.at[n_src + sr], 2, (next_tm, 0)))
     normal = jnp.zeros((48, 128 + lanes), F32)
     for p in range(0, n_tm, 2):
         match = [hot(wanted == vsr[q, 20:21, :]) for q in (p, p + 1)]
@@ -601,6 +565,39 @@
     pl.when(has_next)(lambda: start(right_rows(n_src), br.at[n_src + sr], 5, (next_tm, 0)))
     pl.when(has_prev)(lambda: start(right_rows(n_hi - 1), br.at[n_src + sr], 6, (prev_tm, last_sr)))
 
+    flat_at, plane_at = iota((384, 384), 1), iota((384, 384), 0)
+    mixed = hot(flat_at == 3 * (plane_at & 127) + (plane_at >> 7))
+    flat_ridge = jnp.concatenate([ridge_ref[pl.ds(3 * sr + q, 1), :] for q in range(3)], axis=1)
+    ridge_row = sum(dot_nt(jnp.broadcast_to(part, (16, 384)), mixed)[0:1] for part in pieces_3(flat_ridge))
+    calf[...] = cal_ref[...].astype(F32).reshape(128 * 24, 128)
+    for k in range(24):
+        calp[k] = calf[pl.ds(k, 128, stride=24), :].T
+    for kg in range(6):
+        for lg in range(kg // 2, 3):
+
+            def cal_terms(rows, kg=kg, lg=lg):
+                w = w_ref[rows, :]
+                y = [w * calp[4 * kg + k, rows, :] for k in range(4)]
+                x = [calp[8 * lg + l, rows, :] for l in range(8)]
+                return [y[k] * x[l] for k in range(4) for l in range(8)]
+
+            sums = summed(32, cal_terms)
+            for k in range(4):
+                at = cal_row(4 * kg + k, 8 * lg)
+                vc[at : at + 8, :] = jnp.concatenate(sums[8 * k : 8 * k + 8], axis=0)
+    unit_hot = hot(iota((NCU, 128), 0) == unit_ref[...])
+    unit_hot_2 = jnp.concatenate([unit_hot, unit_hot], axis=1)
+    units = dot_nt(jnp.concatenate(pieces_2(vc[...]), axis=1), unit_hot_2)
+    cp[...] = jnp.concatenate([units[:192], units[192:]], axis=1)
+
+    def cal_share(p):
+        return cp.at[pl.ds(pl.multiple_of(p * share, 8), share)]
+
+    def send_cal(p):
+        pl.when(p < n_own)(lambda: start(cal_share(p), cr.at[sr], 3, (tm, p)))
+
+    other_src(send_cal)
+
     for k in range(5):
         sub[tm, k : k + 1, :] = update[k][:, 128:]
     other_tm(lambda p: start(sub.at[tm], sub.at[tm], 7, (p, sr)))
@@ -629,31 +626,8 @@
     pl.when(has_left)(lambda: start(mown, halo.at[1], 8, (lower // n_src, lower % n_src)))
     pl.when(has_right)(lambda: start(mown, halo.at[0], 9, (upper // n_src, upper % n_src)))
 
-    def sum_cal():
-        cr[sr] = cp[pl.ds(pl.multiple_of(sr * share, 8), share), :]
-        arrived(cr.at[pl.ds(0, last_sr)], 3)
-        total = cr[0]
-        for i in range(1, n_src):
-            total = total + cr[i]
-        c2s[...] = total
-        c2r[tm] = total
-        other_tm(lambda p: start(c2s, c2r.at[tm], 10, (p, sr)))
-
-    pl.when(owner)(sum_cal)
-
     pl.when(has_left)(lambda: arrived(halo.at[0], 9))
     pl.when(has_right)(lambda: arrived(halo.at[1], 8))
-    def finish_cal():
-        arrived(c2r.at[pl.ds(0, last_tm)], 10)
-        total = c2r[0]
-        for i in range(1, n_tm):
-            total = total + c2r[i]
-        c3s[...] = total
-        cf[sr] = total
-        other_src(lambda p: start(c3s, cf.at[sr], 11, (tm, p)))
-
-    pl.when(owner)(finish_cal)
-
     br[sr] = pb[pl.ds(pl.multiple_of(sr * 8, 8), 8), :]
     arrived(br.at[pl.ds(0, last_sr)], 4)
     basis[0] = jnp.zeros((8, 384), F32)
@@ -739,18 +713,17 @@
     )
     xr[pl.ds(pl.multiple_of(sr * XROWS, 8), XROWS), :] = xm[...]
 
-    pl.when(owner)(lambda: arrived(cf.at[pl.ds(0, n_own - 1)], 11))
-    pl.when(jnp.logical_not(owner))(lambda: arrived(cf, 11))
-    packed = jnp.concatenate([cf[i] for i in range(n_own)], axis=0)
-    other_half = pltpu.roll(packed, 64, 1)
-    for k in range(24):
-        size = 24 - 8 * (k // 8)
-        at = cal_row(k, 8 * (k // 8))
-        part = packed[at : at + size] if k < 8 else other_half[at - 192 : at - 192 + size]
-        inv[24 * k + 8 * (k // 8) : 24 * k + 24, :] = part
-    for k in range(8, 24):
-        size = 8 * (k // 8)
-        inv[24 * k : 24 * k + size, :] = inv[pl.ds(k, size, stride=24), :]
+    def sum_cal():
+        cr[sr] = cp[pl.ds(pl.multiple_of(sr * share, 8), share), :]
+        arrived(cr.at[pl.ds(0, last_sr)], 3)
+        total = cr[0]
+        for i in range(1, n_src):
+            total = total + cr[i]
+        c2s[...] = total
+        c2r[tm] = total
+        other_tm(lambda p: start(c2s, c2r.at[tm], 10, (p, sr)))
+
+    pl.when(owner)(sum_cal)
 
     def sweep(j, carry):
         row_of = iota((24, 128), 0)
@@ -765,8 +738,6 @@
         inv[pl.ds(pl.multiple_of(24 * j, 8), 24), :] = jnp.where(row_of == j, -over, scaled)
         return carry
 
-    lax.fori_loop(0, 12, sweep, 0)
-
     arrived(g1.at[pl.ds(0, last_sr)], 12)
     total = g1[0]
     for i in range(1, n_src):
@@ -774,7 +745,17 @@
     gs[1] = total
     g2[tm] = total
     other_tm(lambda p: start(gs.at[1], g2.at[tm], 13, (p, sr)))
-    lax.fori_loop(12, 24, sweep, 0)
+    def finish_cal():
+        arrived(c2r.at[pl.ds(0, last_tm)], 10)
+        total = c2r[0]
+        for i in range(1, n_tm):
+            total = total + c2r[i]
+        c3s[...] = total
+        cf[sr] = total
+        other_src(lambda p: start(c3s, cf.at[sr], 11, (tm, p)))
+
+    pl.when(owner)(finish_cal)
+
     arrived(g2.at[pl.ds(0, last_tm)], 13)
     total = g2[0]
     for i in range(1, n_tm):
@@ -792,7 +773,7 @@
     least = shares[0]
     for value in shares[1:]:
         least = jnp.where(value >= least, least, value)
-    trust_ref[...] = jnp.broadcast_to(jnp.where(least > TRUST, 1.0, 0.0), (8, 128))
+    trust_ref[...] = jnp.where(least > TRUST, 1.0, 0.0)[:, 0:1]
     arrived(sub.at[pl.ds(0, last_tm)], 7)
     for p in range(n_tm):
         update_ref[:, lanes * p : lanes * p + lanes] = sub[p, 0:5, :]
@@ -846,8 +827,24 @@
         for q in range(3):
             att_ref[pl.ds(q, n_src, stride=3), :] = flat[:n_src, 128 * q : 128 * q + 128]
 
-    exchange(kz, nz, zz, 0, lambda p: (tm, p * ny + yy), write_attitude)
-    exchange(ky, ny, yy, 1, lambda p: (tm, zz * ny + p))
+    def start_inverse():
+        write_attitude()
+        pl.when(owner)(lambda: arrived(cf.at[pl.ds(0, n_own - 1)], 11))
+        pl.when(jnp.logical_not(owner))(lambda: arrived(cf, 11))
+        packed = jnp.concatenate([cf[i] for i in range(n_own)], axis=0)
+        other_half = pltpu.roll(packed, 64, 1)
+        for k in range(24):
+            size = 24 - 8 * (k // 8)
+            at = cal_row(k, 8 * (k // 8))
+            part = packed[at : at + size] if k < 8 else other_half[at - 192 : at - 192 + size]
+            inv[24 * k + 8 * (k // 8) : 24 * k + 24, :] = part
+        for k in range(8, 24):
+            size = 8 * (k // 8)
+            inv[24 * k : 24 * k + size, :] = inv[pl.ds(k, size, stride=24), :]
+        lax.fori_loop(0, 12, sweep, 0)
+
+    exchange(kz, nz, zz, 0, lambda p: (tm, p * ny + yy), start_inverse)
+    exchange(ky, ny, yy, 1, lambda p: (tm, zz * ny + p), lambda: lax.fori_loop(12, 24, sweep, 0))
     exchange(kt, n_tm, tm, 2, lambda p: (p, sr))
     total = ks[3]
     right = jnp.concatenate([total[0:8, :NCU], total[0:8, NCU:], total[8:16, :NCU]], axis=0)
@@ -908,11 +905,7 @@
     nz = n_src // ny
     src_planes = jnp.transpose(src_deriv, (1, 2, 0))
     att_planes = jnp.transpose(att_deriv, (1, 2, 0))
-    cal_planes = jnp.transpose(cal_deriv, (1, 2, 0))
-    local_knot = tile_knot - lax.axis_index("tm") * (128 * n_src)
-    meta = jnp.stack([src_id, local_knot, cal_unit] + [jnp.zeros_like(src_id)] * 5)
     ridge = att_ridge.reshape(3 * n_src, 128)
-    prior = jnp.concatenate([src_prior, jnp.ones((3, groups), F32)], axis=0)
 
     def f32(*shape):
         return jax.ShapeDtypeStruct(shape, F32)
@@ -923,13 +916,16 @@
     whole = pl.BlockSpec(memory_space=pltpu.VMEM)
     return pl.pallas_call(
         functools.partial(joint_kernel, n_tm, n_src, n_hi),
-        out_shape=[f32(5, groups), f32(3 * n_src, 128), f32(24, NCU), f32(128, 128), f32(8, 128)],
-        in_specs=[whole] * 9,
+        out_shape=[f32(5, groups), f32(3 * n_src, 128), f32(24, NCU), f32(128, 128), f32(1, 1)],
+        in_specs=[whole] * 11,
         out_specs=[whole] * 5,
         scratch_shapes=[
+            vmem(8, groups),
             vmem(21, 128, 128),
             vmem(5, 128, 128),
+            vmem(12, 128, 128),
             vmem(24, 128, 128),
+            vmem(24 * 128, 128),
             pltpu.VMEM((128, 128), jnp.int32),
             vmem(128, 128),
             vmem(128, 128),
@@ -974,13 +970,36 @@
             collective_id=0, has_side_effects=True, vmem_limit_bytes=48 << 20
         ),
         name="joint_solve",
-    )(src_planes, att_planes, cal_planes, obs_resid, obs_weight, row_offset, meta, prior, ridge)
+    )(src_planes, att_planes, cal_deriv, obs_resid, obs_weight, row_offset, *(a.reshape(1, 128) for a in (src_id, tile_knot, cal_unit)), src_prior, ridge)
+
+
+def hand_over(arrays):
+    count = len(arrays)
+
+    def kernel(*refs):
+        for i in range(count):
+            refs[count + i][...] = refs[i][...]
+
+    whole = pl.BlockSpec(memory_space=pltpu.VMEM)
+    return pl.pallas_call(
+        kernel,
+        out_shape=[jax.ShapeDtypeStruct(a.shape, a.dtype) for a in arrays],
+        in_specs=[whole] * count,
+        out_specs=[whole] * count,
+        name="hand_over",
+    )(*arrays)
 
 
 def guarded_shards(n_tm, n_src, *arrays):
     update, attitude, calib, resid, trust = fast_shards(n_tm, n_src, *arrays)
-    fast = (update, attitude.reshape(-1), calib, resid)
-    return lax.cond(trust[0, 0] > 0.5, lambda: fast, lambda: shards(*arrays))
+    fast = (update, attitude, calib, resid)
+
+    def slow():
+        update, attitude, calib, resid = shards(*arrays)
+        return update, attitude.reshape(-1, 128), calib, resid
+
+    update, attitude, calib, resid = hand_over(lax.cond(trust[0, 0] > 0.5, lambda: fast, slow))
+    return update, attitude.reshape(-1), calib, resid
 
 
 def solution(mesh):

time: 82.4 us -> 77.8 us (0.944)
  local copies, waits for them, and re-layouts: 6.69 us -> 2.46 us
    unnamed x29 -> x20, local copies, waits for them, and re-layouts: 6.14 us -> 2.46 us
    pallas_call x1, Pallas kernels: 73.7 us -> 71.9 us  [fast_shards(): pl.pallas_call(functools.partial(joint_kernel, n_tm, n_src, n_hi), out_sh...]
    pallas_call x0 -> x1, Pallas kernels: none -> 1.55 us  [hand_over(): pl.pallas_call(kernel, out_shape=[jax.ShapeDtypeStruct(a.shape, a.dtype)...]
where the time goes in v1:
time: 77.8 us; the launch traced here: 77.5 us
  Pallas kernels  73.5 us (94%)
  local copies, waits for them, and re-layouts  2.46 us (3%)
  between operations  1.42 us (2%)
    pallas_call x1, Pallas kernels, fast_shards(): pl.pallas_call(functools.partial(joint_kernel, n_tm, n_src, n_hi), out_sh...  71.9 us
    unnamed x20, local copies, waits for them, and re-layouts  2.46 us

profile of v1, /device:TPU:1, one launch (start us, length us, event | category | flops | bytes accessed | tf_op | source)
XLA Modules:
  0.0 77.5 jit_solution(17531002475679474998)
XLA Ops:
  0.6 0.0 copy-start.1
  0.6 0.0 copy-start.66
  0.7 0.0 copy-start.67
  0.7 0.0 copy-start
  0.7 0.0 copy-start.34
  0.7 0.0 copy-start.47
  0.7 0.0 copy-start.42
  0.7 0.0 copy-start.48
  0.7 0.0 copy-start.52
  0.7 1.3 %copy.95 = bf16[128,12,128]{0,2,1:T(8,128)(2,1)S(1)} copy(bf16[128,12,128]{2,0,1:T(8,128)(2,1)} %param.43) | data formatting | bytes 786432 | tf_op args[1]
  2.1 1.1 %copy.94 = bf16[128,5,128]{0,2,1:T(8,128)(2,1)S(1)} copy(bf16[128,5,128]{2,0,1:T(8,128)(2,1)} %param.42) | data formatting | bytes 327680 | tf_op args[0]
  3.2 0.0 copy-done
  3.2 71.9 %joint_solve.1 = (f32[5,1024]{1,0:T(8,128)S(1)}, f32[96,128]{1,0:T(8,128)}, f32[24,64]{1,0:T(8,128)}, f32[128,128]{1,0:T(8,128)}, f32[1,1]{1,0:T(1,128)}) custom-call(bf16[5,128,128]{2,1,0:T(8,128)(2,1)S(1)} %bitcast.216, bf16[12,128,128]{2,1,0:T(8,128)(2,1)S(1)} %bitcast.215, bf16[128,24,128]{2,1,0:T(8,128)(2,1)S(1)} %copy-done, f32[128,128]{1,0:T(8,128)} %resid_in_ref.1, ...), custom_call_target="tpu_custom_call" | custom-call | tf_op jit(solution)/shard_map/joint_solve/pallas_call | solution.py:917
  75.7 0.0 copy-done.1
  75.7 0.0 copy-done.66
  75.7 0.0 copy-done.67
  75.7 0.0 copy-done.34
  75.7 0.0 copy-done.47
  75.7 0.0 copy-done.42
  75.8 0.0 copy-done.48
  75.8 0.0 copy-done.52
  75.8 0.2 conditional.1
  76.0 1.6 %hand_over.1 = (f32[5,1024]{1,0:T(8,128)}, f32[96,128]{1,0:T(8,128)}, f32[24,64]{1,0:T(8,128)}, f32[128,128]{1,0:T(8,128)}) custom-call(f32[5,1024]{1,0:T(8,128)S(1)} %get-tuple-element.826.refs_0_, f32[96,128]{1,0:T(8,128)} %get-tuple-element.827.refs_1_, f32[24,64]{1,0:T(8,128)} %get-tuple-element.828.refs_2_, f32[128,128]{1,0:T(8,128)} %get-tuple-element.829.refs_3_), custom_call_target="tpu_custom_call" | custom-call | tf_op jit(solution)/shard_map/hand_over/pallas_call | solution.py:984
Async XLA Ops:
  0.6 75.1 %copy-start.1 = (bf16[128,5,128]{2,0,1:T(8,128)(2,1)S(1)}, bf16[128,5,128]{2,0,1:T(8,128)(2,1)}, u32[]{:S(2)}) copy-start(bf16[128,5,128]{2,0,1:T(8,128)(2,1)} %param.42) | copy-start | bytes 491524
  0.6 75.1 %copy-start.66 = (s32[128]{0:T(128)S(1)}, s32[128]{0:T(128)}, u32[]{:S(2)}) copy-start(s32[128]{0:T(128)} %param.47) | copy-start | bytes 1540
  0.7 75.1 %copy-start.67 = (s32[128]{0:T(128)S(1)}, s32[128]{0:T(128)}, u32[]{:S(2)}) copy-start(s32[128]{0:T(128)} %param.48) | copy-start | bytes 1540
  0.7 2.5 %copy-start = (bf16[128,24,128]{2,1,0:T(8,128)(2,1)S(1)}, bf16[128,24,128]{2,1,0:T(8,128)(2,1)}, u32[]{:S(2)}) copy-start(bf16[128,24,128]{2,1,0:T(8,128)(2,1)} %cal_ref.1) | copy-start | bytes 2359300
  0.7 75.0 %copy-start.34 = (bf16[128,12,128]{2,0,1:T(8,128)(2,1)S(1)}, bf16[128,12,128]{2,0,1:T(8,128)(2,1)}, u32[]{:S(2)}) copy-start(bf16[128,12,128]{2,0,1:T(8,128)(2,1)} %param.43) | copy-start | bytes 1179652
  0.7 75.0 %copy-start.47 = (f32[128,128]{1,0:T(8,128)S(1)}, f32[128,128]{1,0:T(8,128)}, u32[]{:S(2)}) copy-start(f32[128,128]{1,0:T(8,128)} %resid_in_ref.1) | copy-start | bytes 196612
  0.7 75.0 %copy-start.42 = (f32[128,128]{1,0:T(8,128)S(1)}, f32[128,128]{1,0:T(8,128)}, u32[]{:S(2)}) copy-start(f32[128,128]{1,0:T(8,128)} %weight_ref.1) | copy-start | bytes 196612
  0.7 75.0 %copy-start.48 = (s32[128,128]{1,0:T(8,128)S(1)}, s32[128,128]{1,0:T(8,128)}, u32[]{:S(2)}) copy-start(s32[128,128]{1,0:T(8,128)} %offset_ref.1) | copy-start | bytes 196612
  0.7 75.0 %copy-start.52 = (f32[5,1024]{1,0:T(8,128)S(1)}, f32[5,1024]{1,0:T(8,128)}, u32[]{:S(2)}) copy-start(f32[5,1024]{1,0:T(8,128)} %raw_prior_ref.1) | copy-start | bytes 61444

commit v2 on v1

--- a/solution.py
+++ b/solution.py
@@ -354,7 +354,6 @@
     vrow,
     kz,
     ky,
-    kt,
     ks,
     send,
     recv,
@@ -362,7 +361,6 @@
     tm, sr = lax.axis_index("tm"), lax.axis_index("src")
     last_tm, last_sr = n_tm - 1, n_src - 1
     has_next, has_prev = tm < last_tm, tm > 0
-    first, final = sr == 0, sr == last_sr
     ny = min(4, n_src)
     nz = n_src // ny
     yy, zz = sr % ny, sr // ny
@@ -370,6 +368,16 @@
     n_own = 24 // per_own
     share = 8 * per_own
     owner = sr < n_own
+
+    def block_of(p):
+        return p // ny * ny + (p % ny + p // ny) % ny
+
+    def device_of(b):
+        return b // ny * ny + (b % ny + nz * ny - b // ny) % ny
+
+    block_at = block_of(sr)
+    final_sr = device_of(last_sr)
+    first, final = sr == 0, sr == final_sr
     lanes = prior_ref.shape[1] // n_tm
 
     def start(source, target, at, place):
@@ -417,9 +425,9 @@
     r_ref[...] = resid_in_ref[...].T
     offp[...] = offset_ref[...].astype(F32).T.astype(jnp.int32)
     for k in range(5):
-        srcp[k] = src_ref[k].astype(F32)
+        srcp[k] = src_ref[k].astype(F32).T
     for k in range(12):
-        attp[k] = att_in_ref[k].astype(F32)
+        attp[k] = att_in_ref[k].astype(F32).T
     vm[...] = jnp.zeros_like(vm)
     prior_ref[...] = jnp.ones_like(prior_ref)
     prior_ref[0:5, :] = raw_prior_ref[...]
@@ -475,6 +483,9 @@
                 trace = trace + row
     vs[21:22, :] = trace
 
+    pl.semaphore_wait(barrier, last_tm + last_sr)
+    other_tm(lambda p: start(vs, vsr.at[tm], 0, (p, sr)))
+
     knot = knot_ref[...] - tm * (128 * n_src)
     block, place = knot >> 7, knot & 127
     inside, past = place_lanes(place)
@@ -512,9 +523,7 @@
     owned = dot_nn(jnp.concatenate(pieces_3(prior_ref[...]), axis=0), source_hot)
     owned = owned[0:8] + owned[8:16] + owned[16:24]
 
-    pl.semaphore_wait(barrier, last_tm + last_sr)
-    other_tm(lambda p: start(vs, vsr.at[tm], 0, (p, sr)))
-    other_src(lambda p: start(band_rows(p), mr.at[sr], 1, (tm, p)))
+    other_src(lambda p: start(band_rows(block_of(p)), mr.at[sr], 1, (tm, p)))
 
     vsr[tm] = vs[...]
     arrived(vsr.at[pl.ds(0, last_tm)], 0)
@@ -561,13 +570,13 @@
     def right_rows(j):
         return pb.at[pl.ds(pl.multiple_of(j * 8, 8), 8)]
 
-    other_src(lambda p: start(right_rows(p), br.at[sr], 4, (tm, p)))
+    other_src(lambda p: start(right_rows(block_of(p)), br.at[sr], 4, (tm, p)))
     pl.when(has_next)(lambda: start(right_rows(n_src), br.at[n_src + sr], 5, (next_tm, 0)))
-    pl.when(has_prev)(lambda: start(right_rows(n_hi - 1), br.at[n_src + sr], 6, (prev_tm, last_sr)))
+    pl.when(has_prev)(lambda: start(right_rows(n_hi - 1), br.at[n_src + sr], 6, (prev_tm, final_sr)))
 
     flat_at, plane_at = iota((384, 384), 1), iota((384, 384), 0)
     mixed = hot(flat_at == 3 * (plane_at & 127) + (plane_at >> 7))
-    flat_ridge = jnp.concatenate([ridge_ref[pl.ds(3 * sr + q, 1), :] for q in range(3)], axis=1)
+    flat_ridge = jnp.concatenate([ridge_ref[pl.ds(3 * block_at + q, 1), :] for q in range(3)], axis=1)
     ridge_row = sum(dot_nt(jnp.broadcast_to(part, (16, 384)), mixed)[0:1] for part in pieces_3(flat_ridge))
     calf[...] = cal_ref[...].astype(F32).reshape(128 * 24, 128)
     for k in range(24):
@@ -602,7 +611,7 @@
         sub[tm, k : k + 1, :] = update[k][:, 128:]
     other_tm(lambda p: start(sub.at[tm], sub.at[tm], 7, (p, sr)))
 
-    mr[sr] = mb[pl.ds(pl.multiple_of(sr * MROWS, 8), MROWS), :]
+    mr[sr] = mb[pl.ds(pl.multiple_of(block_at * MROWS, 8), MROWS), :]
     arrived(mr.at[pl.ds(0, last_sr)], 1)
     total = mr[0]
     for i in range(1, n_src):
@@ -620,15 +629,15 @@
     for c in range(3):
         v = SLOT_AT[0, c, c]
         mown[v : v + 1, :] = mown[v : v + 1, :] + ridge_row[:, 128 * c : 128 * c + 128]
-    lin = tm * n_src + sr
+    lin = tm * n_src + block_at
     lower, upper = jnp.maximum(lin - 1, 0), jnp.minimum(lin + 1, n_tm * n_src - 1)
     has_left, has_right = lin > 0, lin < n_tm * n_src - 1
-    pl.when(has_left)(lambda: start(mown, halo.at[1], 8, (lower // n_src, lower % n_src)))
-    pl.when(has_right)(lambda: start(mown, halo.at[0], 9, (upper // n_src, upper % n_src)))
+    pl.when(has_left)(lambda: start(mown, halo.at[1], 8, (lower // n_src, device_of(lower % n_src))))
+    pl.when(has_right)(lambda: start(mown, halo.at[0], 9, (upper // n_src, device_of(upper % n_src))))
 
     pl.when(has_left)(lambda: arrived(halo.at[0], 9))
     pl.when(has_right)(lambda: arrived(halo.at[1], 8))
-    br[sr] = pb[pl.ds(pl.multiple_of(sr * 8, 8), 8), :]
+    br[sr] = pb[pl.ds(pl.multiple_of(block_at * 8, 8), 8), :]
     arrived(br.at[pl.ds(0, last_sr)], 4)
     basis[0] = jnp.zeros((8, 384), F32)
     total = br[0]
@@ -707,11 +716,11 @@
     def slab_rows(i):
         return xr.at[pl.ds(pl.multiple_of(i * XROWS, 8), XROWS)]
 
-    other_src(lambda p: start(xm, slab_rows(sr), 14, (tm, p)))
+    other_src(lambda p: start(xm, slab_rows(block_at), 14, (tm, p)))
     pl.when(has_prev & first)(
         lambda: each(n_src, lambda i: start(xm, slab_rows(n_src), 15, (prev_tm, i)))
     )
-    xr[pl.ds(pl.multiple_of(sr * XROWS, 8), XROWS), :] = xm[...]
+    xr[pl.ds(pl.multiple_of(block_at * XROWS, 8), XROWS), :] = xm[...]
 
     def sum_cal():
         cr[sr] = cp[pl.ds(pl.multiple_of(sr * share, 8), share), :]
@@ -843,10 +852,17 @@
             inv[24 * k : 24 * k + size, :] = inv[pl.ds(k, size, stride=24), :]
         lax.fori_loop(0, 12, sweep, 0)
 
-    exchange(kz, nz, zz, 0, lambda p: (tm, p * ny + yy), start_inverse)
-    exchange(ky, ny, yy, 1, lambda p: (tm, zz * ny + p), lambda: lax.fori_loop(12, 24, sweep, 0))
-    exchange(kt, n_tm, tm, 2, lambda p: (p, sr))
-    total = ks[3]
+    core, xx = tm % 2, tm // 2
+    exchange(kz, 2 * nz, 2 * zz + core, 0, lambda p: (2 * xx + p % 2, p // 2 * ny + yy), start_inverse)
+    exchange(
+        ky,
+        n_tm // 2 * ny,
+        xx * ny + yy,
+        1,
+        lambda p: (p // ny * 2 + core, zz * ny + p % ny),
+        lambda: lax.fori_loop(12, 24, sweep, 0),
+    )
+    total = ks[2]
     right = jnp.concatenate([total[0:8, :NCU], total[0:8, NCU:], total[8:16, :NCU]], axis=0)
     calib = jnp.zeros((24, NCU), F32)
     for j in range(24):
@@ -876,9 +892,8 @@
     left_us(g2.at[pl.ds(0, last_tm)], 13)
     left_us(xr.at[pl.ds(0, XROWS * last_sr)], 14)
     pl.when(has_prev & first)(lambda: left_us(xr.at[pl.ds(0, XROWS * n_src)], 15))
-    left_us(kz.at[pl.ds(0, nz - 1)], 16)
-    left_us(ky.at[pl.ds(0, ny - 1)], 17)
-    left_us(kt.at[pl.ds(0, last_tm)], 18)
+    left_us(kz.at[pl.ds(0, 2 * nz - 1)], 16)
+    left_us(ky.at[pl.ds(0, n_tm // 2 * ny - 1)], 17)
 
 
 def fast_shards(
@@ -903,8 +918,8 @@
     n_own, share = 24 // per_own, 8 * (24 // min(24, n_src))
     ny = min(4, n_src)
     nz = n_src // ny
-    src_planes = jnp.transpose(src_deriv, (1, 2, 0))
-    att_planes = jnp.transpose(att_deriv, (1, 2, 0))
+    src_planes = jnp.transpose(src_deriv, (1, 0, 2))
+    att_planes = jnp.transpose(att_deriv, (1, 0, 2))
     ridge = att_ridge.reshape(3 * n_src, 128)
 
     def f32(*shape):
@@ -959,12 +974,11 @@
             vmem(576, 128),
             vmem(128, 128),
             vmem(24, 128),
-            vmem(nz, 16, 128),
-            vmem(ny, 16, 128),
-            vmem(n_tm, 16, 128),
-            vmem(4, 16, 128),
-            pltpu.SemaphoreType.DMA((19,)),
-            pltpu.SemaphoreType.DMA((19,)),
+            vmem(2 * nz, 16, 128),
+            vmem(n_tm // 2 * ny, 16, 128),
+            vmem(3, 16, 128),
+            pltpu.SemaphoreType.DMA((18,)),
+            pltpu.SemaphoreType.DMA((18,)),
         ],
         compiler_params=pltpu.CompilerParams(
             collective_id=0, has_side_effects=True, vmem_limit_bytes=48 << 20

time: 77.8 us -> 72.6 us (0.933)
  Pallas kernels: 73.5 us -> 70.8 us
  local copies, waits for them, and re-layouts: 2.46 us -> 0.04 us
    pallas_call x1, Pallas kernels: 71.9 us -> 69.2 us  [fast_shards(): pl.pallas_call(functools.partial(joint_kernel, n_tm, n_src, n_hi), out_sh...]
    unnamed x20 -> x18, local copies, waits for them, and re-layouts: 2.46 us -> 0.04 us
where the time goes in v2:
time: 72.6 us; the launch traced here: 72.5 us
  Pallas kernels  70.8 us (98%)
  between operations  1.42 us (2%)
    pallas_call x1, Pallas kernels, fast_shards(): pl.pallas_call(functools.partial(joint_kernel, n_tm, n_src, n_hi), out_sh...  69.2 us
    pallas_call x1, Pallas kernels, hand_over(): pl.pallas_call(kernel, out_shape=[jax.ShapeDtypeStruct(a.shape, a.dtype)...  1.55 us

profile of v2, /device:TPU:1, one launch (start us, length us, event | category | flops | bytes accessed | tf_op | source)
XLA Modules:
  0.0 72.5 jit_solution(6565030292970225026)
XLA Ops:
  0.6 0.0 copy-start.1
  0.6 0.0 copy-start.34
  0.7 0.0 copy-start.66
  0.7 0.0 copy-start.67
  0.7 0.0 copy-start
  0.7 0.0 copy-start.47
  0.7 0.0 copy-start.42
  0.7 0.0 copy-start.48
  0.7 0.0 copy-start.52
  0.7 69.2 %joint_solve.1 = (f32[5,1024]{1,0:T(8,128)S(1)}, f32[96,128]{1,0:T(8,128)}, f32[24,64]{1,0:T(8,128)}, f32[128,128]{1,0:T(8,128)}, f32[1,1]{1,0:T(1,128)}) custom-call(bf16[5,128,128]{2,1,0:T(8,128)(2,1)} %bitcast.221, bf16[12,128,128]{2,1,0:T(8,128)(2,1)} %bitcast.289, bf16[128,24,128]{2,1,0:T(8,128)(2,1)} %cal_ref.1, f32[128,128]{1,0:T(8,128)} %resid_in_ref.1, ...), custom_call_target="tpu_custom_call" | custom-call | tf_op jit(solution)/shard_map/joint_solve/pallas_call | solution.py:932
  70.6 0.0 copy-done.1
  70.6 0.0 copy-done.34
  70.6 0.0 copy-done.66
  70.6 0.0 copy-done.67
  70.6 0.0 copy-done
  70.6 0.0 copy-done.47
  70.7 0.0 copy-done.42
  70.7 0.0 copy-done.48
  70.7 0.0 copy-done.52
  70.7 0.2 conditional.1
  70.9 1.6 %hand_over.1 = (f32[5,1024]{1,0:T(8,128)}, f32[96,128]{1,0:T(8,128)}, f32[24,64]{1,0:T(8,128)}, f32[128,128]{1,0:T(8,128)}) custom-call(f32[5,1024]{1,0:T(8,128)S(1)} %get-tuple-element.826.refs_0_, f32[96,128]{1,0:T(8,128)} %get-tuple-element.827.refs_1_, f32[24,64]{1,0:T(8,128)} %get-tuple-element.828.refs_2_, f32[128,128]{1,0:T(8,128)} %get-tuple-element.829.refs_3_), custom_call_target="tpu_custom_call" | custom-call | tf_op jit(solution)/shard_map/hand_over/pallas_call | solution.py:998
Async XLA Ops:
  0.6 70.0 %copy-start.1 = (bf16[128,5,128]{2,0,1:T(8,128)(2,1)S(1)}, bf16[128,5,128]{2,0,1:T(8,128)(2,1)}, u32[]{:S(2)}) copy-start(bf16[128,5,128]{2,0,1:T(8,128)(2,1)} %param.42) | copy-start | bytes 491524
  0.6 70.0 %copy-start.34 = (bf16[128,12,128]{2,0,1:T(8,128)(2,1)S(1)}, bf16[128,12,128]{2,0,1:T(8,128)(2,1)}, u32[]{:S(2)}) copy-start(bf16[128,12,128]{2,0,1:T(8,128)(2,1)} %param.43) | copy-start | bytes 1179652
  0.7 70.0 %copy-start.66 = (s32[128]{0:T(128)S(1)}, s32[128]{0:T(128)}, u32[]{:S(2)}) copy-start(s32[128]{0:T(128)} %param.47) | copy-start | bytes 1540
  0.7 70.0 %copy-start.67 = (s32[128]{0:T(128)S(1)}, s32[128]{0:T(128)}, u32[]{:S(2)}) copy-start(s32[128]{0:T(128)} %param.48) | copy-start | bytes 1540
  0.7 70.0 %copy-start = (bf16[128,24,128]{2,1,0:T(8,128)(2,1)S(1)}, bf16[128,24,128]{2,1,0:T(8,128)(2,1)}, u32[]{:S(2)}) copy-start(bf16[128,24,128]{2,1,0:T(8,128)(2,1)} %cal_ref.1) | copy-start | bytes 2359300
  0.7 70.0 %copy-start.47 = (f32[128,128]{1,0:T(8,128)S(1)}, f32[128,128]{1,0:T(8,128)}, u32[]{:S(2)}) copy-start(f32[128,128]{1,0:T(8,128)} %resid_in_ref.1) | copy-start | bytes 196612
  0.7 70.0 %copy-start.42 = (f32[128,128]{1,0:T(8,128)S(1)}, f32[128,128]{1,0:T(8,128)}, u32[]{:S(2)}) copy-start(f32[128,128]{1,0:T(8,128)} %weight_ref.1) | copy-start | bytes 196612
  0.7 70.0 %copy-start.48 = (s32[128,128]{1,0:T(8,128)S(1)}, s32[128,128]{1,0:T(8,128)}, u32[]{:S(2)}) copy-start(s32[128,128]{1,0:T(8,128)} %offset_ref.1) | copy-start | bytes 196612
  0.7 70.0 %copy-start.52 = (f32[5,1024]{1,0:T(8,128)S(1)}, f32[5,1024]{1,0:T(8,128)}, u32[]{:S(2)}) copy-start(f32[5,1024]{1,0:T(8,128)} %raw_prior_ref.1) | copy-start | bytes 61444

commit v3 on v2

--- a/solution.py
+++ b/solution.py
@@ -204,7 +204,7 @@
 BF16 = jnp.bfloat16
 MESH = pl.DeviceIdType.MESH
 MROWS = 32
-XROWS = 24
+XROWS = 18
 TRUST = 0.01
 
 
@@ -411,7 +411,7 @@
 
     next_tm, prev_tm = jnp.minimum(tm + 1, last_tm), jnp.maximum(tm - 1, 0)
     halo[...] = jnp.zeros_like(halo)
-    xr[XROWS * n_src :, :] = jnp.zeros((XROWS * (n_hi - n_src), 128), F32)
+    xr[n_src:] = jnp.zeros((n_hi - n_src, XROWS, 128), F32)
 
     barrier = pltpu.get_barrier_semaphore()
 
@@ -505,15 +505,24 @@
         right = jnp.concatenate(pieces_2(spread) + pieces_2(over), axis=1)
         return dot_nt(spreads, right)[:n_hi]
 
+    def band_rows(j, at=0, size=MROWS):
+        return mb.at[pl.ds(pl.multiple_of(j * MROWS + at, 8), size)]
+
+    half = MROWS // 2
     for v, (delta, c, d) in enumerate(SLOTS):
         rows = spread_rows(lambda m, v=v: vm[m, v : v + 1, :], 7 - delta)
         if v < MROWS:
             mb[pl.ds(v, n_hi, stride=MROWS), :] = rows
+            if v + 1 in (half, MROWS):
+                at, sem = v + 1 - half, 1 if v < half else 18
+                other_src(
+                    lambda p, at=at, sem=sem: start(
+                        band_rows(block_of(p), at, half), mr.at[sr, pl.ds(at, half)], sem, (tm, p)
+                    )
+                )
         else:
             ex[...] = rows
 
-    def band_rows(j):
-        return mb.at[pl.ds(pl.multiple_of(j * MROWS, 8), MROWS)]
 
     ids = jnp.broadcast_to(id_ref[...].astype(F32), (128, 128)).T
     sources = (iota((lanes, 128), 0) + tm * lanes).astype(F32)
@@ -523,7 +532,6 @@
     owned = dot_nn(jnp.concatenate(pieces_3(prior_ref[...]), axis=0), source_hot)
     owned = owned[0:8] + owned[8:16] + owned[16:24]
 
-    other_src(lambda p: start(band_rows(block_of(p)), mr.at[sr], 1, (tm, p)))
 
     vsr[tm] = vs[...]
     arrived(vsr.at[pl.ds(0, last_tm)], 0)
@@ -612,7 +620,8 @@
     other_tm(lambda p: start(sub.at[tm], sub.at[tm], 7, (p, sr)))
 
     mr[sr] = mb[pl.ds(pl.multiple_of(block_at * MROWS, 8), MROWS), :]
-    arrived(mr.at[pl.ds(0, last_sr)], 1)
+    arrived(mr.at[pl.ds(0, last_sr), pl.ds(0, half)], 1)
+    arrived(mr.at[pl.ds(0, last_sr), pl.ds(0, half)], 18)
     total = mr[0]
     for i in range(1, n_src):
         total = total + mr[i]
@@ -708,19 +717,28 @@
     same = iota((32, 128), 0) == iota((32, 128), 1)
     sums = jnp.sum(jnp.where(in_gram, gt[...], 0.0), axis=1, keepdims=True)
     gs[0] = jnp.broadcast_to(jnp.sum(jnp.where(same, sums, 0.0), axis=0, keepdims=True), (8, 128))
-    g1[sr] = gs[0]
-    other_src(lambda p: start(gs.at[0], g1.at[sr], 12, (tm, p)))
+    core, xx = tm % 2, tm // 2
+    g1[2 * zz + core] = gs[0]
+    each(
+        2 * nz - 1,
+        lambda d: start(
+            gs.at[0],
+            g1.at[2 * zz + core],
+            12,
+            (2 * xx + (2 * zz + core + 1 + d) % 2, (2 * zz + core + 1 + d) % (2 * nz) // 2 * ny + yy),
+        ),
+    )
     for k in range(CG_ITERS):
         xm[3 * k : 3 * k + 3, :] = own[k][0:3]
 
     def slab_rows(i):
-        return xr.at[pl.ds(pl.multiple_of(i * XROWS, 8), XROWS)]
+        return xr.at[i]
 
     other_src(lambda p: start(xm, slab_rows(block_at), 14, (tm, p)))
     pl.when(has_prev & first)(
         lambda: each(n_src, lambda i: start(xm, slab_rows(n_src), 15, (prev_tm, i)))
     )
-    xr[pl.ds(pl.multiple_of(block_at * XROWS, 8), XROWS), :] = xm[...]
+    xr[block_at] = xm[...]
 
     def sum_cal():
         cr[sr] = cp[pl.ds(pl.multiple_of(sr * share, 8), share), :]
@@ -747,13 +765,23 @@
         inv[pl.ds(pl.multiple_of(24 * j, 8), 24), :] = jnp.where(row_of == j, -over, scaled)
         return carry
 
-    arrived(g1.at[pl.ds(0, last_sr)], 12)
+    arrived(g1.at[pl.ds(0, 2 * nz - 1)], 12)
     total = g1[0]
-    for i in range(1, n_src):
+    for i in range(1, 2 * nz):
         total = total + g1[i]
     gs[1] = total
-    g2[tm] = total
-    other_tm(lambda p: start(gs.at[1], g2.at[tm], 13, (p, sr)))
+    n_xy = n_tm // 2 * ny
+    at_xy = xx * ny + yy
+    g2[at_xy] = total
+    each(
+        n_xy - 1,
+        lambda d: start(
+            gs.at[1],
+            g2.at[at_xy],
+            13,
+            ((at_xy + 1 + d) % n_xy // ny * 2 + core, zz * ny + (at_xy + 1 + d) % n_xy % ny),
+        ),
+    )
     def finish_cal():
         arrived(c2r.at[pl.ds(0, last_tm)], 10)
         total = c2r[0]
@@ -765,9 +793,9 @@
 
     pl.when(owner)(finish_cal)
 
-    arrived(g2.at[pl.ds(0, last_tm)], 13)
+    arrived(g2.at[pl.ds(0, n_xy - 1)], 13)
     total = g2[0]
-    for i in range(1, n_tm):
+    for i in range(1, n_xy):
         total = total + g2[i]
     sums = jnp.sum(jnp.where(same, total[0:1], 0.0), axis=1, keepdims=True)
     gt[...] = jnp.broadcast_to(sums, (32, 128))
@@ -789,14 +817,14 @@
 
     here_3 = jnp.concatenate([here[:n_hi].astype(F32)] * 3 + [jnp.zeros((128 - 3 * n_hi, 128), F32)], axis=0).astype(BF16)
     after_3 = jnp.concatenate([after[:n_hi].astype(F32)] * 3 + [jnp.zeros((128 - 3 * n_hi, 128), F32)], axis=0).astype(BF16)
-    arrived(xr.at[pl.ds(0, XROWS * last_sr)], 14)
+    arrived(xr.at[pl.ds(0, last_sr)], 14)
     pl.when(has_next)(lambda: arrived(slab_rows(n_src), 15))
     resid_b = ra[...]
     planes = []
     for c in range(3):
-        plane = weights[0] * xr[pl.ds(c, n_hi, stride=XROWS), :]
+        plane = weights[0] * xr[:, c, :]
         for k in range(1, CG_ITERS):
-            plane = plane + weights[k] * xr[pl.ds(3 * k + c, n_hi, stride=XROWS), :]
+            plane = plane + weights[k] * xr[:, 3 * k + c, :]
         planes.append(plane)
         parts = [part.astype(F32) for part in pieces_3(plane)]
         parts.append(jnp.zeros((128 - 3 * n_hi, 128), F32))
@@ -812,8 +840,7 @@
     for k in range(24):
         vrow[k : k + 1, :] = jnp.sum(calp[k] * weighted, axis=0, keepdims=True)
     units = dot_nt(jnp.concatenate(pieces_2(vrow[...]), axis=1), unit_hot_2)
-    ks[0, 0:8, :] = jnp.concatenate([units[0:8], units[8:16]], axis=1)
-    ks[0, 8:16, :] = jnp.concatenate([units[16:24], jnp.zeros((8, NCU), F32)], axis=1)
+    ks[0] = jnp.concatenate([units[0:12], units[12:24]], axis=1)
 
     def exchange(buffer, count, me, at, place, beside=None):
         buffer[me] = ks[at]
@@ -863,7 +890,7 @@
         lambda: lax.fori_loop(12, 24, sweep, 0),
     )
     total = ks[2]
-    right = jnp.concatenate([total[0:8, :NCU], total[0:8, NCU:], total[8:16, :NCU]], axis=0)
+    right = jnp.concatenate([total[:, :NCU], total[:, NCU:]], axis=0)
     calib = jnp.zeros((24, NCU), F32)
     for j in range(24):
         calib = calib - inv[24 * j : 24 * j + 24, :NCU] * right[j : j + 1]
@@ -876,7 +903,8 @@
     resid_ref[...] = out.T
 
     left_us(vsr.at[pl.ds(0, last_tm)], 0)
-    left_us(mr.at[pl.ds(0, last_sr)], 1)
+    left_us(mr.at[pl.ds(0, last_sr), pl.ds(0, half)], 1)
+    left_us(mr.at[pl.ds(0, last_sr), pl.ds(0, half)], 18)
     pl.when(has_next)(lambda: left_us(mr.at[0], 2))
     pl.when(owner)(lambda: left_us(cr.at[pl.ds(0, n_own - 1)], 3))
     pl.when(jnp.logical_not(owner))(lambda: left_us(cr.at[pl.ds(0, n_own)], 3))
@@ -888,10 +916,10 @@
     pl.when(has_right)(lambda: left_us(mown, 9))
     pl.when(owner)(lambda: left_us(c2r.at[pl.ds(0, last_tm)], 10))
     pl.when(owner)(lambda: left_us(cr.at[pl.ds(0, last_sr)], 11))
-    left_us(g1.at[pl.ds(0, last_sr)], 12)
-    left_us(g2.at[pl.ds(0, last_tm)], 13)
-    left_us(xr.at[pl.ds(0, XROWS * last_sr)], 14)
-    pl.when(has_prev & first)(lambda: left_us(xr.at[pl.ds(0, XROWS * n_src)], 15))
+    left_us(g1.at[pl.ds(0, 2 * nz - 1)], 12)
+    left_us(g2.at[pl.ds(0, n_xy - 1)], 13)
+    left_us(xr.at[pl.ds(0, last_sr)], 14)
+    pl.when(has_prev & first)(lambda: left_us(xr.at[pl.ds(0, n_src)], 15))
     left_us(kz.at[pl.ds(0, 2 * nz - 1)], 16)
     left_us(ky.at[pl.ds(0, n_tm // 2 * ny - 1)], 17)
 
@@ -960,11 +988,11 @@
             vmem(CG_ITERS + 2, 8, 384),
             vmem(CG_ITERS, 8, 128),
             vmem(2, 8, 128),
-            vmem(n_src, 8, 128),
-            vmem(n_tm, 8, 128),
+            vmem(2 * nz, 8, 128),
+            vmem(n_tm // 2 * ny, 8, 128),
             vmem(32, 128),
             vmem(XROWS, 128),
-            vmem(n_hi * XROWS, 128),
+            vmem(n_hi, XROWS, 128),
             vmem(n_tm, 8, lanes),
             vmem(n_src, share, 128),
             vmem(share, 128),
@@ -974,11 +1002,11 @@
             vmem(576, 128),
             vmem(128, 128),
             vmem(24, 128),
-            vmem(2 * nz, 16, 128),
-            vmem(n_tm // 2 * ny, 16, 128),
-            vmem(3, 16, 128),
-            pltpu.SemaphoreType.DMA((18,)),
-            pltpu.SemaphoreType.DMA((18,)),
+            vmem(2 * nz, 12, 128),
+            vmem(n_tm // 2 * ny, 12, 128),
+            vmem(3, 12, 128),
+            pltpu.SemaphoreType.DMA((19,)),
+            pltpu.SemaphoreType.DMA((19,)),
         ],
         compiler_params=pltpu.CompilerParams(
             collective_id=0, has_side_effects=True, vmem_limit_bytes=48 << 20

time: 72.6 us -> 67.4 us (0.928)
  Pallas kernels: 70.8 us -> 65.5 us
    pallas_call x1, Pallas kernels: 69.2 us -> 63.9 us  [fast_shards(): pl.pallas_call(functools.partial(joint_kernel, n_tm, n_src, n_hi), out_sh...]
where the time goes in v3:
time: 67.4 us; the launch traced here: 67.1 us
  Pallas kernels  65.5 us (97%)
  between operations  1.42 us (2%)
    pallas_call x1, Pallas kernels, fast_shards(): pl.pallas_call(functools.partial(joint_kernel, n_tm, n_src, n_hi), out_sh...  63.9 us
    pallas_call x1, Pallas kernels, hand_over(): pl.pallas_call(kernel, out_shape=[jax.ShapeDtypeStruct(a.shape, a.dtype)...  1.55 us

profile of v3, /device:TPU:1, one launch (start us, length us, event | category | flops | bytes accessed | tf_op | source)
XLA Modules:
  0.0 67.1 jit_solution(16149043668539427105)
XLA Ops:
  0.6 0.0 copy-start.1
  0.6 0.0 copy-start.34
  0.7 0.0 copy-start.66
  0.7 0.0 copy-start.67
  0.7 0.0 copy-start
  0.7 0.0 copy-start.47
  0.7 0.0 copy-start.42
  0.7 0.0 copy-start.48
  0.7 0.0 copy-start.52
  0.7 63.9 %joint_solve.1 = (f32[5,1024]{1,0:T(8,128)S(1)}, f32[96,128]{1,0:T(8,128)}, f32[24,64]{1,0:T(8,128)}, f32[128,128]{1,0:T(8,128)}, f32[1,1]{1,0:T(1,128)}) custom-call(bf16[5,128,128]{2,1,0:T(8,128)(2,1)} %bitcast.221, bf16[12,128,128]{2,1,0:T(8,128)(2,1)} %bitcast.289, bf16[128,24,128]{2,1,0:T(8,128)(2,1)} %cal_ref.1, f32[128,128]{1,0:T(8,128)} %resid_in_ref.1, ...), custom_call_target="tpu_custom_call" | custom-call | tf_op jit(solution)/shard_map/joint_solve/pallas_call | solution.py:960
  65.3 0.0 copy-done.1
  65.3 0.0 copy-done.34
  65.3 0.0 copy-done.66
  65.3 0.0 copy-done.67
  65.3 0.0 copy-done
  65.4 0.0 copy-done.47
  65.4 0.0 copy-done.42
  65.4 0.0 copy-done.48
  65.4 0.0 copy-done.52
  65.4 0.2 conditional.1
  65.6 1.6 %hand_over.1 = (f32[5,1024]{1,0:T(8,128)}, f32[96,128]{1,0:T(8,128)}, f32[24,64]{1,0:T(8,128)}, f32[128,128]{1,0:T(8,128)}) custom-call(f32[5,1024]{1,0:T(8,128)S(1)} %get-tuple-element.826.refs_0_, f32[96,128]{1,0:T(8,128)} %get-tuple-element.827.refs_1_, f32[24,64]{1,0:T(8,128)} %get-tuple-element.828.refs_2_, f32[128,128]{1,0:T(8,128)} %get-tuple-element.829.refs_3_), custom_call_target="tpu_custom_call" | custom-call | tf_op jit(solution)/shard_map/hand_over/pallas_call | solution.py:1026
Async XLA Ops:
  0.6 64.7 %copy-start.1 = (bf16[128,5,128]{2,0,1:T(8,128)(2,1)S(1)}, bf16[128,5,128]{2,0,1:T(8,128)(2,1)}, u32[]{:S(2)}) copy-start(bf16[128,5,128]{2,0,1:T(8,128)(2,1)} %param.42) | copy-start | bytes 491524
  0.6 64.7 %copy-start.34 = (bf16[128,12,128]{2,0,1:T(8,128)(2,1)S(1)}, bf16[128,12,128]{2,0,1:T(8,128)(2,1)}, u32[]{:S(2)}) copy-start(bf16[128,12,128]{2,0,1:T(8,128)(2,1)} %param.43) | copy-start | bytes 1179652
  0.7 64.7 %copy-start.66 = (s32[128]{0:T(128)S(1)}, s32[128]{0:T(128)}, u32[]{:S(2)}) copy-start(s32[128]{0:T(128)} %param.47) | copy-start | bytes 1540
  0.7 64.7 %copy-start.67 = (s32[128]{0:T(128)S(1)}, s32[128]{0:T(128)}, u32[]{:S(2)}) copy-start(s32[128]{0:T(128)} %param.48) | copy-start | bytes 1540
  0.7 64.7 %copy-start = (bf16[128,24,128]{2,1,0:T(8,128)(2,1)S(1)}, bf16[128,24,128]{2,1,0:T(8,128)(2,1)}, u32[]{:S(2)}) copy-start(bf16[128,24,128]{2,1,0:T(8,128)(2,1)} %cal_ref.1) | copy-start | bytes 2359300
  0.7 64.7 %copy-start.47 = (f32[128,128]{1,0:T(8,128)S(1)}, f32[128,128]{1,0:T(8,128)}, u32[]{:S(2)}) copy-start(f32[128,128]{1,0:T(8,128)} %resid_in_ref.1) | copy-start | bytes 196612
  0.7 64.7 %copy-start.42 = (f32[128,128]{1,0:T(8,128)S(1)}, f32[128,128]{1,0:T(8,128)}, u32[]{:S(2)}) copy-start(f32[128,128]{1,0:T(8,128)} %weight_ref.1) | copy-start | bytes 196612
  0.7 64.7 %copy-start.48 = (s32[128,128]{1,0:T(8,128)S(1)}, s32[128,128]{1,0:T(8,128)}, u32[]{:S(2)}) copy-start(s32[128,128]{1,0:T(8,128)} %offset_ref.1) | copy-start | bytes 196612
  0.7 64.7 %copy-start.52 = (f32[5,1024]{1,0:T(8,128)S(1)}, f32[5,1024]{1,0:T(8,128)}, u32[]{:S(2)}) copy-start(f32[5,1024]{1,0:T(8,128)} %raw_prior_ref.1) | copy-start | bytes 61444

commit v4 on v3

--- a/solution.py
+++ b/solution.py
@@ -586,35 +586,6 @@
     mixed = hot(flat_at == 3 * (plane_at & 127) + (plane_at >> 7))
     flat_ridge = jnp.concatenate([ridge_ref[pl.ds(3 * block_at + q, 1), :] for q in range(3)], axis=1)
     ridge_row = sum(dot_nt(jnp.broadcast_to(part, (16, 384)), mixed)[0:1] for part in pieces_3(flat_ridge))
-    calf[...] = cal_ref[...].astype(F32).reshape(128 * 24, 128)
-    for k in range(24):
-        calp[k] = calf[pl.ds(k, 128, stride=24), :].T
-    for kg in range(6):
-        for lg in range(kg // 2, 3):
-
-            def cal_terms(rows, kg=kg, lg=lg):
-                w = w_ref[rows, :]
-                y = [w * calp[4 * kg + k, rows, :] for k in range(4)]
-                x = [calp[8 * lg + l, rows, :] for l in range(8)]
-                return [y[k] * x[l] for k in range(4) for l in range(8)]
-
-            sums = summed(32, cal_terms)
-            for k in range(4):
-                at = cal_row(4 * kg + k, 8 * lg)
-                vc[at : at + 8, :] = jnp.concatenate(sums[8 * k : 8 * k + 8], axis=0)
-    unit_hot = hot(iota((NCU, 128), 0) == unit_ref[...])
-    unit_hot_2 = jnp.concatenate([unit_hot, unit_hot], axis=1)
-    units = dot_nt(jnp.concatenate(pieces_2(vc[...]), axis=1), unit_hot_2)
-    cp[...] = jnp.concatenate([units[:192], units[192:]], axis=1)
-
-    def cal_share(p):
-        return cp.at[pl.ds(pl.multiple_of(p * share, 8), share)]
-
-    def send_cal(p):
-        pl.when(p < n_own)(lambda: start(cal_share(p), cr.at[sr], 3, (tm, p)))
-
-    other_src(send_cal)
-
     for k in range(5):
         sub[tm, k : k + 1, :] = update[k][:, 128:]
     other_tm(lambda p: start(sub.at[tm], sub.at[tm], 7, (p, sr)))
@@ -643,6 +614,35 @@
     has_left, has_right = lin > 0, lin < n_tm * n_src - 1
     pl.when(has_left)(lambda: start(mown, halo.at[1], 8, (lower // n_src, device_of(lower % n_src))))
     pl.when(has_right)(lambda: start(mown, halo.at[0], 9, (upper // n_src, device_of(upper % n_src))))
+
+    calf[...] = cal_ref[...].astype(F32).reshape(128 * 24, 128)
+    for k in range(24):
+        calp[k] = calf[pl.ds(k, 128, stride=24), :].T
+    for kg in range(6):
+        for lg in range(kg // 2, 3):
+
+            def cal_terms(rows, kg=kg, lg=lg):
+                w = w_ref[rows, :]
+                y = [w * calp[4 * kg + k, rows, :] for k in range(4)]
+                x = [calp[8 * lg + l, rows, :] for l in range(8)]
+                return [y[k] * x[l] for k in range(4) for l in range(8)]
+
+            sums = summed(32, cal_terms)
+            for k in range(4):
+                at = cal_row(4 * kg + k, 8 * lg)
+                vc[at : at + 8, :] = jnp.concatenate(sums[8 * k : 8 * k + 8], axis=0)
+    unit_hot = hot(iota((NCU, 128), 0) == unit_ref[...])
+    unit_hot_2 = jnp.concatenate([unit_hot, unit_hot], axis=1)
+    units = dot_nt(jnp.concatenate(pieces_2(vc[...]), axis=1), unit_hot_2)
+    cp[...] = jnp.concatenate([units[:192], units[192:]], axis=1)
+
+    def cal_share(p):
+        return cp.at[pl.ds(pl.multiple_of(p * share, 8), share)]
+
+    def send_cal(p):
+        pl.when(p < n_own)(lambda: start(cal_share(p), cr.at[sr], 3, (tm, p)))
+
+    other_src(send_cal)
 
     pl.when(has_left)(lambda: arrived(halo.at[0], 9))
     pl.when(has_right)(lambda: arrived(halo.at[1], 8))

time: 67.4 us -> 70.8 us (1.050)
  Pallas kernels: 65.5 us -> 69 us
    pallas_call x1, Pallas kernels: 63.9 us -> 67.4 us  [fast_shards(): pl.pallas_call(functools.partial(joint_kernel, n_tm, n_src, n_hi), out_sh...]
where the time goes in v4:
time: 70.8 us; the launch traced here: 70.6 us
  Pallas kernels  69 us (97%)
  between operations  1.42 us (2%)
    pallas_call x1, Pallas kernels, fast_shards(): pl.pallas_call(functools.partial(joint_kernel, n_tm, n_src, n_hi), out_sh...  67.4 us
    pallas_call x1, Pallas kernels, hand_over(): pl.pallas_call(kernel, out_shape=[jax.ShapeDtypeStruct(a.shape, a.dtype)...  1.55 us

profile of v4, /device:TPU:1, one launch (start us, length us, event | category | flops | bytes accessed | tf_op | source)
XLA Modules:
  0.0 70.6 jit_solution(4264304844176968565)
XLA Ops:
  0.6 0.0 copy-start.1
  0.6 0.0 copy-start.34
  0.7 0.0 copy-start.66
  0.7 0.0 copy-start.67
  0.7 0.0 copy-start
  0.7 0.0 copy-start.47
  0.7 0.0 copy-start.42
  0.7 0.0 copy-start.48
  0.7 0.0 copy-start.52
  0.7 67.4 %joint_solve.1 = (f32[5,1024]{1,0:T(8,128)S(1)}, f32[96,128]{1,0:T(8,128)}, f32[24,64]{1,0:T(8,128)}, f32[128,128]{1,0:T(8,128)}, f32[1,1]{1,0:T(1,128)}) custom-call(bf16[5,128,128]{2,1,0:T(8,128)(2,1)} %bitcast.221, bf16[12,128,128]{2,1,0:T(8,128)(2,1)} %bitcast.289, bf16[128,24,128]{2,1,0:T(8,128)(2,1)} %cal_ref.1, f32[128,128]{1,0:T(8,128)} %resid_in_ref.1, ...), custom_call_target="tpu_custom_call" | custom-call | tf_op jit(solution)/shard_map/joint_solve/pallas_call | solution.py:960
  68.8 0.0 copy-done.1
  68.8 0.0 copy-done.34
  68.8 0.0 copy-done.66
  68.8 0.0 copy-done.67
  68.8 0.0 copy-done
  68.8 0.0 copy-done.47
  68.9 0.0 copy-done.42
  68.9 0.0 copy-done.48
  68.9 0.0 copy-done.52
  68.9 0.2 conditional.1
  69.1 1.6 %hand_over.1 = (f32[5,1024]{1,0:T(8,128)}, f32[96,128]{1,0:T(8,128)}, f32[24,64]{1,0:T(8,128)}, f32[128,128]{1,0:T(8,128)}) custom-call(f32[5,1024]{1,0:T(8,128)S(1)} %get-tuple-element.826.refs_0_, f32[96,128]{1,0:T(8,128)} %get-tuple-element.827.refs_1_, f32[24,64]{1,0:T(8,128)} %get-tuple-element.828.refs_2_, f32[128,128]{1,0:T(8,128)} %get-tuple-element.829.refs_3_), custom_call_target="tpu_custom_call" | custom-call | tf_op jit(solution)/shard_map/hand_over/pallas_call | solution.py:1026
Async XLA Ops:
  0.6 68.2 %copy-start.1 = (bf16[128,5,128]{2,0,1:T(8,128)(2,1)S(1)}, bf16[128,5,128]{2,0,1:T(8,128)(2,1)}, u32[]{:S(2)}) copy-start(bf16[128,5,128]{2,0,1:T(8,128)(2,1)} %param.42) | copy-start | bytes 491524
  0.6 68.2 %copy-start.34 = (bf16[128,12,128]{2,0,1:T(8,128)(2,1)S(1)}, bf16[128,12,128]{2,0,1:T(8,128)(2,1)}, u32[]{:S(2)}) copy-start(bf16[128,12,128]{2,0,1:T(8,128)(2,1)} %param.43) | copy-start | bytes 1179652
  0.7 68.2 %copy-start.66 = (s32[128]{0:T(128)S(1)}, s32[128]{0:T(128)}, u32[]{:S(2)}) copy-start(s32[128]{0:T(128)} %param.47) | copy-start | bytes 1540
  0.7 68.2 %copy-start.67 = (s32[128]{0:T(128)S(1)}, s32[128]{0:T(128)}, u32[]{:S(2)}) copy-start(s32[128]{0:T(128)} %param.48) | copy-start | bytes 1540
  0.7 68.2 %copy-start = (bf16[128,24,128]{2,1,0:T(8,128)(2,1)S(1)}, bf16[128,24,128]{2,1,0:T(8,128)(2,1)}, u32[]{:S(2)}) copy-start(bf16[128,24,128]{2,1,0:T(8,128)(2,1)} %cal_ref.1) | copy-start | bytes 2359300
  0.7 68.2 %copy-start.47 = (f32[128,128]{1,0:T(8,128)S(1)}, f32[128,128]{1,0:T(8,128)}, u32[]{:S(2)}) copy-start(f32[128,128]{1,0:T(8,128)} %resid_in_ref.1) | copy-start | bytes 196612
  0.7 68.2 %copy-start.42 = (f32[128,128]{1,0:T(8,128)S(1)}, f32[128,128]{1,0:T(8,128)}, u32[]{:S(2)}) copy-start(f32[128,128]{1,0:T(8,128)} %weight_ref.1) | copy-start | bytes 196612
  0.7 68.2 %copy-start.48 = (s32[128,128]{1,0:T(8,128)S(1)}, s32[128,128]{1,0:T(8,128)}, u32[]{:S(2)}) copy-start(s32[128,128]{1,0:T(8,128)} %offset_ref.1) | copy-start | bytes 196612
  0.7 68.2 %copy-start.52 = (f32[5,1024]{1,0:T(8,128)S(1)}, f32[5,1024]{1,0:T(8,128)}, u32[]{:S(2)}) copy-start(f32[5,1024]{1,0:T(8,128)} %raw_prior_ref.1) | copy-start | bytes 61444
